TPU v7x, 128 devices: a whole 4x4x4 slice. The times are simulated.
128 devices in a mesh: dp: 4 (over y_hi, core), fsdp: 32 (over y_lo, x, z).
Axes of the slice: x: 4, y: 4 (y_hi: 2, y_lo: 2; y = y_hi * 2 + y_lo), z: 4, core: 2. Of those that a mesh axis runs over, the one named last changes fastest.
Arguments:
- activations: bfloat16 [2048, 8192], P('dp', 'fsdp'), may hold values from -6 to 6
- out_grads: bfloat16 [2048, 8192], P('dp', 'fsdp'), may hold values from -6 to 6
- query_acts: bfloat16 [128, 8192], P(None, 'fsdp'), may hold values from -6 to 6
- query_grads: bfloat16 [128, 8192], P(None, 'fsdp'), may hold values from -6 to 6
- eig_in: bfloat16 [8192, 8192], P('fsdp'), may hold values from -0.125 to 0.125
- eig_out: bfloat16 [8192, 8192], P('fsdp'), may hold values from -0.0625 to 0.0625
- example_ids: int32 [4, 512], P('dp'), may hold values from 0 to 7, never falling along the last dimension, each value on 1 to 128 neighbouring positions
Outputs:
- corrections: float32 [8192, 8192], P('fsdp')
- scores: float32 [32, 32], P(None, 'dp')
Inputs may be any that keep to these rules, and one draw needn't show every extreme that they name: `example_ids`: in each group's row the ids never fall, every QA pair 0 to 7 has 1 to 128 tokens, and one has exactly 128.
All inputs are finite; a program needn't handle non-finite values.
Results may differ from a plain program's by a relative error of at most 0.0055.
Values may be sent and summed in bfloat16 or wider, within the bound.
A program may use at most 192 MiB of HBM per device.

v0:
```python
import jax
import jax.numpy as jnp
from jax import lax
from jax.sharding import PartitionSpec as P

D_IN = 8192
D_OUT = 8192
MOST = 128
EX = 8
NQ = 32
QTOK = 4


def per_device(activations, out_grads, query_acts, query_grads, eig_in, eig_out, example_ids):
    f32 = jnp.float32
    tok_count = activations.shape[0]
    rows_in = jnp.concatenate([activations, query_acts], axis=0)
    k_local = eig_in.shape[0]
    rot_in = lax.psum_scatter(
        lax.dot_general(eig_in, rows_in, (((0,), (1,)), ((), ())), preferred_element_type=f32),
        "fsdp",
        scatter_dimension=0,
        tiled=True,
    )
    rot_in = rot_in.astype(jnp.bfloat16)
    rows_out = jnp.concatenate([out_grads, query_grads], axis=0)
    rot_local = lax.dot_general(
        lax.all_gather(rows_out, "fsdp", axis=1, tiled=True),
        eig_out,
        (((1,), (1,)), ((), ())),
        preferred_element_type=f32,
    )
    rot_out = lax.all_gather(rot_local.astype(jnp.bfloat16), "fsdp", axis=1, tiled=True)
    ids_row = example_ids[0]
    numbers = jnp.arange(EX, dtype=jnp.int32)
    member = ids_row[None, :] == numbers[:, None]
    starts = jnp.sum((ids_row[None, :] < numbers[:, None]).astype(jnp.int32), axis=1)
    starts = jnp.minimum(starts, tok_count - MOST)
    row_index = starts[:, None] + jnp.arange(MOST, dtype=jnp.int32)[None, :]
    live_rows = jnp.take_along_axis(member, row_index, axis=1)
    out_rows = rot_out[row_index]
    out_rows = jnp.where(live_rows[:, :, None], out_rows, jnp.zeros_like(out_rows))
    in_cols = rot_in[:, row_index]
    rotated = jnp.einsum("kem,emi->eki", in_cols, out_rows, preferred_element_type=f32).astype(
        jnp.bfloat16
    )
    wide = rotated.astype(f32)
    squares = jnp.sum(wide * wide, axis=0)
    summed = lax.psum(squares, "dp")
    whole_sum = lax.psum(jnp.sum(summed), "fsdp")
    pair_count = EX * lax.axis_size("dp")
    corrections = summed / pair_count
    damping = 0.5 * (whole_sum / pair_count) / (jnp.float32(D_IN) * jnp.float32(D_OUT))
    precond = (wide / (corrections + damping)[None]).astype(jnp.bfloat16)
    query_out = rot_out[tok_count:]
    query_in = rot_in[:, tok_count:]
    partial_value = jnp.einsum("eki,ti->ekt", precond, query_out, preferred_element_type=f32)
    weighted = partial_value * query_in[None].astype(f32)
    per_query = jnp.sum(weighted.reshape(EX, k_local, NQ, QTOK), axis=(1, 3))
    norm_factor = 1.0 / jnp.sqrt(jnp.float32(D_IN) * jnp.float32(D_OUT))
    scores = lax.psum(per_query.T * norm_factor, "fsdp")
    return (corrections, scores)


def solution(mesh):
    return jax.shard_map(
        per_device,
        mesh=mesh,
        in_specs=(
            P("dp", "fsdp"),
            P("dp", "fsdp"),
            P(None, "fsdp"),
            P(None, "fsdp"),
            P("fsdp", None),
            P("fsdp", None),
            P("dp", None),
        ),
        out_specs=(P("fsdp", None), P(None, "dp")),
        check_vma=False,
    )
```

profile of v0, /device:TPU:0, one launch (start us, length us, event | category | flops | bytes accessed | tf_op | source)
XLA Modules:
  0.0 1107.5 jit_solution(13968103552690041796)
XLA Ops:
  7.2 0.0 all-gather.3.cloned.1.call-start
  7.2 1.8 pad_maximum_fusion
  9.0 0.0 all-gather.3.cloned.1.call-update
  9.0 0.0 all-gather.5.cloned.1.call-start
  9.1 193.8 %all-gather.3.cloned.1.call-done = bf16[640,8192]{1,0:T(8,128)(2,1)} async-done(((bf16[640,256]{1,0:T(8,128)(2,1)}), bf16[640,8192]{1,0:T(8,128)(2,1)}) %all-gather.3.cloned.1.call-update) | async-done | bytes 10485776 | tf_op jit(solution)/shard_map/all_gather | solution.py:28
  202.9 8.8 convolution_convert_fusion.1
  211.7 0.0 all-gather.5.cloned.1.call-update
  211.7 0.0 reduce-scatter.2.cloned.1.call-start
  211.8 10.8 convolution_bitcast_fusion
  222.7 0.2 all-reduce.2.cloned.1.call-start
  222.9 0.4 copy-done.2
  223.3 0.1 convert_reduce_fusion
  223.5 0.1 fusion.22
  223.6 8.8 gather_fusion.2
  232.3 0.1 fusion.26
  232.4 0.1 fusion.18
  232.5 173.4 %all-gather.5.cloned.1.call-done = bf16[640,8192]{1,0:T(8,128)(2,1)} async-done(((bf16[640,256]{1,0:T(8,128)(2,1)}), bf16[640,8192]{1,0:T(8,128)(2,1)}) %all-gather.5.cloned.1.call-update) | async-done | bytes 10485776 | tf_op jit(solution)/shard_map/all_gather | solution.py:33
  405.8 33.2 %gather_fusion.1 = bf16[1024,8192]{1,0:T(8,128)(2,1)} fusion(bf16[640,8192]{1,0:T(8,128)(2,1)} %all-gather.5.cloned.1.call-done, s32[1024]{0:T(1024)S(1)} %fusion.18), kind=kCustom, calls=%fused_computation.1 | custom fusion | bytes 33558528 | tf_op jit(solution)/shard_map/gather | solution.py:41
  439.0 203.2 %reduce-scatter.2.cloned.1.call-done = f32[256,640]{0,1:T(8,128)} async-done(((f32[8192,640]{0,1:T(8,128)}), f32[256,640]{0,1:T(8,128)}) %reduce-scatter.2.cloned.1.call-update) | async-done | bytes 655376 | tf_op jit(solution)/shard_map/reduce_scatter | solution.py:19
  642.2 1.1 convert_element_type.22
  643.3 3.9 gather_fusion
  647.3 0.3 copy.13
  647.6 24.9 %fusion = (f32[256,8192]{1,0:T(8,128)}, bf16[8,256,8192]{2,1,0:T(8,128)(2,1)}) fusion(bf16[8,128,8192]{2,1,0:T(8,128)(2,1)} %bitcast.31, pred[8,128]{1,0:T(8,128)(4,1)S(1)} %fusion.26, bf16[8,128,256]{1,2,0:T(8,128)(2,1)S(1)} %copy.13), kind=kOutput, calls=%fused_computation.5 | convolution fusion | flops 4368367616 | bytes 59245568 | tf_op jit(solution)/shard_map/kem,emi->eki/dot_general | solution.py:44
  672.5 157.4 %all-reduce.2.cloned.1.call-done = f32[256,8192]{1,0:T(8,128)} async-done(((f32[256,8192]{1,0:T(8,128)}), f32[256,8192]{1,0:T(8,128)}) %all-reduce.2.cloned.1.call-update) | async-done | bytes 8388624 | tf_op jit(solution)/shard_map/psum | solution.py:49
  829.9 6.1 reduce_sum.45
  836.1 0.1 copy.14
  836.1 82.8 %psum.22 = f32[]{:T(128)} all-reduce(f32[]{:T(128)} %reduce_sum.45), channel_id=1, replica_groups=mesh['dp'=4,'fsdp'=32] {'fsdp'}, use_global_device_ids=true, to_apply=%region_5.6 | all-reduce | flops 1 | bytes 8 | tf_op jit(solution)/shard_map/psum | solution.py:50
  919.6 11.4 %broadcast_add_fusion = (f32[256,8192]{1,0:T(8,128)}, f32[256,8192]{1,0:T(8,128)}) fusion(f32[]{:T(128)S(6)} %div.20, f32[256,8192]{1,0:T(8,128)} %all-reduce.2.cloned.1.call-done), kind=kLoop, calls=%fused_computation.13 | loop fusion | flops 4194304 | bytes 25165828 | tf_op jit(solution)/shard_map/add | solution.py:54
  931.0 17.1 %fusion.10 = f32[8,128]{1,0:T(8,128)S(1)} fusion(bf16[640,8192]{1,0:T(8,128)(2,1)} %all-gather.5.cloned.1.call-done, bf16[8,256,8192]{2,1,0:T(8,128)(2,1)} %get-tuple-element.7, f32[256,8192]{1,0:T(8,128)} %get-tuple-element.4, f32[256,128]{1,0:T(8,128)S(1)} %copy.14), kind=kOutput, calls=%fused_computation.18 | convolution fusion | flops 4345822208 | bytes 44175360 | tf_op jit(solution)/shard_map/eki,ti->ekt/dot_general | solution.py:57
  948.0 0.1 copy.15
  948.2 152.1 %psum.23 = f32[32,8]{1,0:T(8,128)S(1)} all-reduce(f32[32,8]{1,0:T(8,128)S(1)} %multiply_bitcast_fusion), channel_id=1, replica_groups=mesh['dp'=4,'fsdp'=32] {'fsdp'}, use_global_device_ids=true, to_apply=%region_8.9 | all-reduce | flops 256 | bytes 2048 | tf_op jit(solution)/shard_map/psum | solution.py:61
  1100.3 0.7 copy.16
  (12 shorter events, 0.1 us)
Async XLA Ops:
  7.2 204.6 %copy-start.1 = (bf16[128,256]{1,0:T(8,128)(2,1)S(1)}, bf16[128,256]{1,0:T(8,128)(2,1)}, u32[]{:S(2)}) copy-start(bf16[128,256]{1,0:T(8,128)(2,1)} %param.9) | copy-start | bytes 196612
  7.2 204.6 %copy-start = (bf16[512,256]{1,0:T(8,128)(2,1)S(1)}, bf16[512,256]{1,0:T(8,128)(2,1)}, u32[]{:S(2)}) copy-start(bf16[512,256]{1,0:T(8,128)(2,1)} %param.7) | copy-start | bytes 786436
  7.2 195.7 %all-gather.3.cloned.1.call-start = ((), (), s32[]{:S(2)}) async-start(), calls=%async_computation.2 | async-start | bytes 10813440 | tf_op jit(solution)/shard_map/all_gather | solution.py:28
  9.0 396.8 %all-gather.5.cloned.1.call-start = ((), (), s32[]{:S(2)}) async-start(), calls=%async_computation.3 | async-start | bytes 10813440 | tf_op jit(solution)/shard_map/all_gather | solution.py:33
  211.7 430.5 %reduce-scatter.2.cloned.1.call-start = ((), (), s32[]{:S(2)}) async-start(), calls=%async_computation.1 | async-start | bytes 21626880 | tf_op jit(solution)/shard_map/reduce_scatter | solution.py:19
  222.7 0.7 copy-start.2
  222.7 607.2 %all-reduce.2.cloned.1.call-start = ((), (), s32[]{:S(2)}) async-start(), calls=%async_computation.4 | async-start | bytes 16777216 | tf_op jit(solution)/shard_map/psum | solution.py:49
Sparse Core Ops, SparseCore 0:
  10.2 192.7 all-gather.2
  211.9 193.9 all-gather.4
  408.2 233.9 reduce-scatter.1
  672.6 157.2 all-reduce.1
where the time goes:
time: 1110 us
  waiting for transfers between devices  728 us (66%)
  blocking collectives  235 us (21%)
  matrix products  61.6 us (6%)
  local copies, waits for them, and re-layouts  47.5 us (4%)
  other arithmetic  20.8 us (2%)
  between operations  14.5 us (1%)
    reduce_scatter x1, waiting for transfers between devices, per_device(): lax.psum_scatter(lax.dot_general(eig_in, rows_in, (((0,), (1,)), ((), ())...  203 us
    all_gather x1, waiting for transfers between devices, per_device(): lax.all_gather(rows_out, 'fsdp', axis=1, tiled=True)  194 us
    all_gather x1, waiting for transfers between devices, per_device(): lax.all_gather(rot_local.astype(jnp.bfloat16), 'fsdp', axis=1, tiled=True)  173 us
    psum x1, waiting for transfers between devices, per_device(): summed = lax.psum(squares, 'dp')  157 us
    psum x1, blocking collectives, per_device(): scores = lax.psum(per_query.T * norm_factor, 'fsdp')  152 us
    psum x1, blocking collectives, per_device(): whole_sum = lax.psum(jnp.sum(summed), 'fsdp')  82.8 us
    gather x1, local copies, waits for them, and re-layouts, per_device(): out_rows = rot_out[row_index]  33.2 us
    dot_general x1, matrix products, per_device(): jnp.einsum('kem,emi->eki', in_cols, out_rows, preferred_element_type=f32)  24.9 us
  transfers between devices with their start and end apart: 4, of which 4 were waited for; matrix products, arithmetic and copies ran while one was open for 5% of the time, Pallas kernels for 0%

commit v1 on v0

v1 whole, which is shorter than its diff:
```python
import jax
import jax.numpy as jnp
from jax import lax
from jax.experimental import pallas as pl
from jax.experimental.pallas import tpu as pltpu
from jax.sharding import PartitionSpec as P

D_IN = 8192
D_OUT = 8192
EX = 8
NQ = 32
QTOK = 4
ROWS = 1152
MESH = pl.DeviceIdType.MESH
F32 = jnp.float32
BF16 = jnp.bfloat16


def place():
    dp, fs = lax.axis_index("dp"), lax.axis_index("fsdp")
    return dp // 2, lax.rem(dp, 2), fs // 16, lax.rem(fs // 4, 4), lax.rem(fs, 4)


def device(h, c, y, x, z):
    return (2 * h + c, 16 * y + 4 * x + z)


def greet(partners):
    barrier = pltpu.get_barrier_semaphore()
    for partner in partners:
        pl.semaphore_signal(barrier, 1, device_id=partner, device_id_type=MESH)
    pl.semaphore_wait(barrier, len(partners))


def remote(src, dst, sems, slot, target):
    return pltpu.make_async_remote_copy(
        src_ref=src, dst_ref=dst, send_sem=sems[0].at[slot], recv_sem=sems[1].at[slot],
        device_id=target, device_id_type=MESH,
    )


def rotate_kernel(
    act, grd, qa, qg, eig_in, eig_out, x_out, y_out,
    a_buf, g_buf, u_buf, v_buf,
    xs_buf, xr_buf, vs_buf, vr_buf, xys_buf, xyr_buf, vys_buf, vyr_buf, x_own, v_own,
    loc, h_s, h_r, ag_s, ag_r, gg_s, gg_r, u_s, u_r, v_s, v_r, us_s, us_r, vsib_s, vsib_r,
    x_s, x_r, z_s, z_r, y_s, y_r,
):
    h, c, y, x, z = place()
    oh, oc, oy = 1 - h, 1 - c, 1 - y
    xs = [lax.rem(x + d, 4) for d in range(4)]
    zs = [lax.rem(z + d, 4) for d in range(4)]
    sibling = device(h, oc, y, x, z)
    greet(
        [sibling, device(oh, c, y, x, z), device(h, c, oy, x, z)]
        + [device(h, c, y, xs[d], z) for d in (1, 2, 3)]
        + [device(h, c, y, x, zs[d]) for d in (1, 2, 3)]
        + [device(h, c, oy, x, zs[d]) for d in (1, 2, 3)]
    )
    started = []

    def go(copy):
        copy.start()
        started.append(copy)
        return copy

    ah = go(remote(act, a_buf.at[z, pl.ds(640, 512)], (h_s, h_r), 0, device(oh, c, y, x, z)))
    gh = go(remote(grd, g_buf.at[x, pl.ds(640, 512)], (h_s, h_r), 1, device(oh, c, y, x, z)))
    local = [
        pltpu.make_async_copy(act, a_buf.at[z, pl.ds(0, 512)], loc.at[0]),
        pltpu.make_async_copy(qa, a_buf.at[z, pl.ds(512, 128)], loc.at[1]),
        pltpu.make_async_copy(grd, g_buf.at[x, pl.ds(0, 512)], loc.at[2]),
        pltpu.make_async_copy(qg, g_buf.at[x, pl.ds(512, 128)], loc.at[3]),
    ]
    for copy in local:
        copy.start()
    own = []
    for p in range(4):
        own.append(pltpu.make_async_copy(
            eig_in.at[:, pl.ds(256 * (16 * h + 4 * p + z), 256)], u_buf.at[z, p], loc.at[4 + p]))
        own.append(pltpu.make_async_copy(
            eig_out.at[pl.ds(128 * h, 128), pl.ds(256 * (16 * y + 4 * p + z), 256)],
            v_buf.at[z, p, pl.ds(128 * y, 128)], loc.at[8 + p]))
    for copy in own:
        copy.start()
    for copy in local:
        copy.wait()
    a1, g1 = [], []
    for d in (1, 3, 2):
        mine = pl.ds(0, 640)
        a1.append(go(remote(a_buf.at[z, mine], a_buf.at[z, mine], (ag_s, ag_r), d, device(h, c, y, x, zs[d]))))
        g1.append(go(remote(g_buf.at[x, mine], g_buf.at[x, mine], (gg_s, gg_r), d, device(h, c, y, xs[d], z))))
    u1, v1 = [], []
    for d in (1, 3, 2):
        for p in range(2):
            piece = 2 * c + p
            u1.append(go(remote(
                eig_in.at[:, pl.ds(256 * (16 * h + 4 * piece + zs[d]), 256)], u_buf.at[z, piece],
                (u_s, u_r), 2 * d + p, device(h, c, y, x, zs[d]))))
    for dy, yd in ((0, y), (1, oy)):
        for d in (1, 3, 2, 0):
            if dy == 0 and d == 0:
                continue
            for p in range(2):
                piece = 2 * c + p
                v1.append((dy, d, p, go(remote(
                    eig_out.at[pl.ds(128 * h, 128), pl.ds(256 * (16 * yd + 4 * piece + zs[d]), 256)],
                    v_buf.at[z, piece, pl.ds(128 * y, 128)],
                    (v_s, v_r), 8 * dy + 2 * d + p, device(h, c, yd, x, zs[d])))))
    ah.wait_recv()
    gh.wait_recv()
    other = pl.ds(640, 512)
    for d in (1, 3, 2):
        a1.append(go(remote(a_buf.at[z, other], a_buf.at[z, other], (ag_s, ag_r), 4 + d, device(h, c, y, x, zs[d]))))
        g1.append(go(remote(g_buf.at[x, other], g_buf.at[x, other], (gg_s, gg_r), 4 + d, device(h, c, y, xs[d], z))))
    handed = []
    for n, d in enumerate((1, 3, 2)):
        src = lax.rem(z + 4 - d, 4)
        for p in range(2):
            u1[2 * n + p].wait_recv()
        part = u_buf.at[src, pl.ds(2 * c, 2)]
        handed.append(go(remote(part, part, (us_s, us_r), d, sibling)))
    for copy in own:
        copy.wait()
    for copy in a1:
        copy.wait_recv()
    for copy in handed:
        copy.wait_recv()
    tile = 384
    xsend = []

    def product_in(piece, store):
        def body(i, _):
            rows = pl.ds(pl.multiple_of(i * tile, tile), tile)
            total = jnp.zeros((tile, 256), F32)
            for s in range(4):
                total += jnp.dot(a_buf[s, rows, :], u_buf[s, piece], preferred_element_type=F32)
            store(rows, total)
            return 0
        lax.fori_loop(0, ROWS // tile, body, 0)

    for n, d in enumerate((1, 3, 2, 0)):
        if d:
            def store(rows, total):
                xs_buf[n, rows, :] = total.astype(BF16)
            product_in(xs[d], store)
            xsend.append(go(remote(xs_buf.at[n], xr_buf.at[n], (x_s, x_r), n, device(h, c, y, xs[d], z))))
        else:
            def store(rows, total):
                x_own[rows, :] = total
            product_in(xs[0], store)
    vhanded = []
    arrived = {}
    for dy, d, p, copy in v1:
        copy.wait_recv()
        arrived[(dy, d)] = arrived.get((dy, d), 0) + 1
        if arrived[(dy, d)] == 2:
            src = lax.rem(z + 4 - d, 4)
            part = v_buf.at[src, pl.ds(2 * c, 2), pl.ds(128 * (y if dy == 0 else oy), 128)]
            vhanded.append(go(remote(part, part, (vsib_s, vsib_r), 4 * dy + d, sibling)))
    for copy in g1:
        copy.wait_recv()
    for copy in vhanded:
        copy.wait_recv()
    zsend = []

    def product_out(piece, store):
        def body(i, _):
            rows = pl.ds(pl.multiple_of(i * tile, tile), tile)
            total = jnp.zeros((tile, 256), F32)
            for s in range(4):
                total += lax.dot_general(
                    g_buf[s, rows, :], v_buf[piece, s], (((1,), (1,)), ((), ())), preferred_element_type=F32)
            store(rows, total)
            return 0
        lax.fori_loop(0, ROWS // tile, body, 0)

    for n, d in enumerate((1, 3, 2, 0)):
        if d:
            def store(rows, total):
                vs_buf[n, rows, :] = total.astype(BF16)
            product_out(zs[d], store)
            zsend.append(go(remote(vs_buf.at[n], vr_buf.at[n], (z_s, z_r), n, device(h, c, y, x, zs[d]))))
        else:
            def store(rows, total):
                v_own[rows, :] = total
            product_out(zs[0], store)

    def add_up(own_ref, got, send):
        def body(i, _):
            rows = pl.ds(pl.multiple_of(i * 128, 128), 128)
            total = own_ref[rows, :]
            for n in range(3):
                total += got[n, rows, :].astype(F32)
            own_ref[rows, :] = total
            send[rows, :] = jnp.where(y == 0, total[:, 128:], total[:, :128]).astype(BF16)
            return 0
        lax.fori_loop(0, ROWS // 128, body, 0)

    partner = device(h, c, oy, x, z)
    for copy in xsend:
        copy.wait_recv()
    add_up(x_own, xr_buf, xys_buf)
    xy = go(remote(xys_buf, xyr_buf, (y_s, y_r), 0, partner))
    for copy in zsend:
        copy.wait_recv()
    add_up(v_own, vr_buf, vys_buf)
    vy = go(remote(vys_buf, vyr_buf, (y_s, y_r), 1, partner))

    def block_at(n):
        return jnp.where(n < 4, 4 * h + n, jnp.where(n == 4, 8, 4 * oh + n - 5))

    def finish(own_ref, got, out, turn):
        def body(i, _):
            rows = pl.ds(pl.multiple_of(i * 128, 128), 128)
            total = own_ref[rows, :]
            mine = jnp.where(y == 0, total[:, :128], total[:, 128:]) + got[rows, :].astype(F32)
            out[block_at(i)] = (mine.T if turn else mine).astype(BF16)
            return 0
        lax.fori_loop(0, 9, body, 0)

    xy.wait_recv()
    finish(x_own, xyr_buf, x_out, True)
    vy.wait_recv()
    finish(v_own, vyr_buf, y_out, False)
    for copy in started:
        copy.wait_send()


def rotate(act, grd, qa, qg, eig_in, eig_out):
    dma = pltpu.SemaphoreType.DMA
    any_ = pl.BlockSpec(memory_space=pl.ANY)
    vmem = pl.BlockSpec(memory_space=pltpu.VMEM)
    return pl.pallas_call(
        rotate_kernel,
        out_shape=(jax.ShapeDtypeStruct((9, 128, 128), BF16), jax.ShapeDtypeStruct((9, 128, 128), BF16)),
        in_specs=[any_] * 6,
        out_specs=(vmem, vmem),
        scratch_shapes=[
            pltpu.VMEM((4, ROWS, 256), BF16),
            pltpu.VMEM((4, ROWS, 256), BF16),
            pltpu.VMEM((4, 4, 256, 256), BF16),
            pltpu.VMEM((4, 4, 256, 256), BF16),
            pltpu.VMEM((3, ROWS, 256), BF16),
            pltpu.VMEM((3, ROWS, 256), BF16),
            pltpu.VMEM((3, ROWS, 256), BF16),
            pltpu.VMEM((3, ROWS, 256), BF16),
            pltpu.VMEM((ROWS, 128), BF16),
            pltpu.VMEM((ROWS, 128), BF16),
            pltpu.VMEM((ROWS, 128), BF16),
            pltpu.VMEM((ROWS, 128), BF16),
            pltpu.VMEM((ROWS, 256), F32),
            pltpu.VMEM((ROWS, 256), F32),
            dma((12,)),
            dma((2,)), dma((2,)),
            dma((8,)), dma((8,)),
            dma((8,)), dma((8,)),
            dma((8,)), dma((8,)),
            dma((16,)), dma((16,)),
            dma((4,)), dma((4,)),
            dma((8,)), dma((8,)),
            dma((3,)), dma((3,)),
            dma((3,)), dma((3,)),
            dma((2,)), dma((2,)),
        ],
        compiler_params=pltpu.CompilerParams(
            collective_id=1, has_side_effects=True, vmem_limit_bytes=40 * 2**20),
        cost_estimate=pl.CostEstimate(flops=5 * 10**9, bytes_accessed=10**7, transcendentals=0),
        name="rotate",
    )(act, grd, qa, qg, eig_in, eig_out)


def score_kernel(
    x_mine, y_mine, ids, corr, scores,
    x_all, y_all, id_all, rot, sq, sq_got, c_stage, acc, red, red_got, red2, red2_got, blks,
    loc, gx_s, gx_r, gy_s, gy_r, id_s, id_r, sq_s, sq_r, t_s, t_r, o_s, o_r, f_s, f_r, p_s, p_r,
):
    h, c, y, x, z = place()
    oh, oc, oy = 1 - h, 1 - c, 1 - y
    yy = 2 * h + y
    xs = [lax.rem(x + d, 4) for d in range(4)]
    zs = [lax.rem(z + d, 4) for d in range(4)]
    ys = [lax.rem(yy + d, 4) for d in range(4)]
    sibling = device(h, oc, y, x, z)

    def at_y(v):
        return device(v // 2, c, lax.rem(v, 2), x, z)

    plane = []
    for dy in range(4):
        for dx in range(4):
            if dy or dx:
                plane.append(device(ys[dy] // 2, c, lax.rem(ys[dy], 2), xs[dx], z))
    greet([sibling] + plane + [device(h, c, y, x, zs[d]) for d in (1, 2, 3)])
    started = []

    def go(copy):
        copy.start()
        started.append(copy)
        return copy

    def x_slot(xv, yv):
        return x_all.at[:, pl.ds(pl.multiple_of(128 * (2 * xv + yv), 128), 128), :]

    def y_slot(zv, hv):
        return y_all.at[:, :, pl.ds(pl.multiple_of(128 * (2 * zv + hv), 128), 128)]

    across_h, across_y = device(oh, c, y, x, z), device(h, c, oy, x, z)
    ids_copy = go(remote(ids, id_all.at[h], (id_s, id_r), 0, across_h))
    xy = go(remote(x_mine, x_slot(x, y), (gx_s, gx_r), 0, across_y))
    yh = go(remote(y_mine, y_slot(z, h), (gy_s, gy_r), 0, across_h))
    got = []
    for d in (1, 3, 2):
        got.append(go(remote(x_mine, x_slot(x, y), (gx_s, gx_r), d, device(h, c, y, xs[d], z))))
        got.append(go(remote(y_mine, y_slot(z, h), (gy_s, gy_r), d, device(h, c, y, x, zs[d]))))
    local = [
        pltpu.make_async_copy(x_mine, x_slot(x, y), loc.at[0]),
        pltpu.make_async_copy(y_mine, y_slot(z, h), loc.at[1]),
        pltpu.make_async_copy(ids, id_all.at[h], loc.at[2]),
    ]
    for copy in local:
        copy.start()
    xy.wait_recv()
    for d in (1, 3, 2):
        got.append(go(remote(x_slot(x, oy), x_slot(x, oy), (gx_s, gx_r), 4 + d, device(h, c, y, xs[d], z))))
    yh.wait_recv()
    for d in (1, 3, 2):
        got.append(go(remote(y_slot(z, oh), y_slot(z, oh), (gy_s, gy_r), 4 + d, device(h, c, y, x, zs[d]))))
    for copy in local:
        copy.wait()
    ids_copy.wait_recv()
    for g in range(2):
        row = id_all[g]
        for e in range(EX):
            first = jnp.sum((row < e).astype(jnp.int32))
            blks[8 * g + e] = jnp.minimum(first // 128, 2)
    for copy in got:
        copy.wait_recv()

    def quarter(kt, _):
        rows = pl.ds(pl.multiple_of(256 * kt, 256), 256)

        def pair(n, _):
            g, e = n // 8, lax.rem(n, 8)
            blk = blks[n]
            parts = []
            for b in range(2):
                keep = id_all[g, blk + b] == e
                parts.append(jnp.where(keep, x_all[4 * g + blk + b, rows, :].astype(F32), 0.0).astype(BF16))
            left = jnp.concatenate(parts, axis=1)
            for it in range(2):
                cols = pl.ds(512 * it, 512)
                right = jnp.concatenate(
                    [y_all[4 * g + blk, :, cols], y_all[4 * g + blk + 1, :, cols]], axis=0)
                value = jnp.dot(left, right, preferred_element_type=F32).astype(BF16)
                rot[n, rows, cols] = value
                wide = value.astype(F32)

                @pl.when(n == 0)
                def _():
                    sq[kt, :, cols] = wide * wide

                @pl.when(n > 0)
                def _():
                    sq[kt, :, cols] += wide * wide
            return 0

        lax.fori_loop(0, 2 * EX, pair, 0)
        copy = remote(sq.at[kt], sq_got.at[kt], (sq_s, sq_r), kt, sibling)
        copy.start()
        return 0

    lax.fori_loop(0, 4, quarter, 0)

    def add_up(kt, total):
        copy = remote(sq.at[kt], sq_got.at[kt], (sq_s, sq_r), kt, sibling)
        copy.wait()

        def chunk(i, total):
            part = pl.ds(pl.multiple_of(32 * i, 32), 32)
            value = (sq[kt, part, :] + sq_got[kt, part, :]) * (1.0 / 32.0)
            sq[kt, part, :] = value
            for a in range(4):
                for b in range(8):
                    total = total + value[8 * a:8 * a + 8, 128 * b:128 * b + 128]
            return total

        total = lax.fori_loop(0, 8, chunk, total)
        c_stage[kt] = sq[kt, pl.ds(pl.multiple_of(128 * c, 128), 128), :].astype(BF16)
        return total

    total = lax.fori_loop(0, 4, add_up, jnp.zeros((8, 128), F32))

    def spread(value, n, buf, got_buf, sems, where):
        buf[n] = value
        copies = [go(remote(buf.at[n], got_buf.at[n, d - 1], sems, 3 * n + d - 1, where(d))) for d in (1, 2, 3)]
        for copy in copies:
            copy.wait_recv()
        return buf[n] + got_buf[n, 0] + got_buf[n, 1] + got_buf[n, 2]

    steps = (
        lambda d: device(h, c, y, x, zs[d]),
        lambda d: device(h, c, y, xs[d], z),
        lambda d: at_y(ys[d]),
    )
    for n in range(3):
        total = spread(total, n, red, red_got, (t_s, t_r), steps[n])
    damping = 0.5 * (jnp.sum(total) / (float(D_IN) * float(D_OUT)))

    def slab(yv, xv):
        return corr.at[pl.ds(pl.multiple_of(128 * c, 128), 128),
                       pl.ds(pl.multiple_of(1024 * (4 * yv + xv), 1024), 1024)]

    me = 4 * y + x

    def is_me(hv, xv):
        return jnp.logical_and(jnp.logical_and(hv == h, h == y), xv == x)

    def hand_out(start):
        for hd in range(2):
            for d in range(4):
                hv, xv = (h, oh)[hd], xs[d]
                slot = 4 * hd + d
                copy = pltpu.make_async_remote_copy(
                    src_ref=c_stage.at[xv], dst_ref=slab(y, x), send_sem=o_s.at[slot], recv_sem=o_r.at[me],
                    device_id=device(hv, c, h, xv, z), device_id_type=MESH)
                run = copy.start if start else copy.wait_send
                if hd == 0 and d == 0:
                    @pl.when(h != y)
                    def _():
                        run()

                    @pl.when(h == y)
                    def _():
                        own = pltpu.make_async_copy(c_stage.at[x], slab(y, x), loc.at[3])
                        if start:
                            own.start()
                        else:
                            own.wait()
                else:
                    run()

    hand_out(True)

    def second(kt, _):
        rows = pl.ds(pl.multiple_of(256 * kt, 256), 256)

        def invert(i, _):
            part = pl.ds(pl.multiple_of(32 * i, 32), 32)
            sq[kt, part, :] = 1.0 / (sq[kt, part, :] + damping)
            return 0

        lax.fori_loop(0, 8, invert, 0)
        query_in = x_all[8, rows, :].astype(F32)

        def pair(n, _):
            cond = (rot[n, rows, :].astype(F32) * sq[kt]).astype(BF16)
            part = lax.dot_general(
                cond, y_all[8], (((1,), (1,)), ((), ())), preferred_element_type=F32)
            weighted = part * query_in
            value = jnp.sum(weighted, axis=0, keepdims=True)

            @pl.when(kt == 0)
            def _():
                acc[pl.ds(n, 1), :] = value

            @pl.when(kt > 0)
            def _():
                acc[pl.ds(n, 1), :] += value
            return 0

        lax.fori_loop(0, 2 * EX, pair, 0)
        return 0

    lax.fori_loop(0, 4, second, 0)
    hand_out(False)

    def forward(i, _):
        yv, xv = i // 4, lax.rem(i, 4)
        mine = jnp.logical_and(h == y, i == me)

        @pl.when(jnp.logical_not(mine))
        def _():
            pltpu.make_async_remote_copy(
                src_ref=c_stage.at[0], dst_ref=slab(yv, xv), send_sem=o_s.at[0], recv_sem=o_r.at[i],
                device_id=sibling, device_id_type=MESH).wait_recv()
        pltpu.make_async_remote_copy(
            src_ref=slab(yv, xv), dst_ref=slab(yv, xv), send_sem=f_s.at[i], recv_sem=f_r.at[i],
            device_id=sibling, device_id_type=MESH).start()
        return 0

    lax.fori_loop(0, 8, forward, 0)
    value = acc[...]
    for n in range(3):
        value = spread(value, n, red2, red2_got, (p_s, p_r), steps[n])
    scores[...] = value

    def last(i, _):
        yv, xv = i // 4, lax.rem(i, 4)
        pltpu.make_async_remote_copy(
            src_ref=slab(yv, xv), dst_ref=slab(yv, xv), send_sem=f_s.at[i], recv_sem=f_r.at[i],
            device_id=sibling, device_id_type=MESH).wait()
        return 0

    lax.fori_loop(0, 8, last, 0)
    for copy in started:
        copy.wait_send()


def score(x_mine, y_mine, ids):
    dma = pltpu.SemaphoreType.DMA
    vmem = pl.BlockSpec(memory_space=pltpu.VMEM)
    return pl.pallas_call(
        score_kernel,
        out_shape=(jax.ShapeDtypeStruct((256, D_OUT), BF16), jax.ShapeDtypeStruct((2 * EX, 128), F32)),
        in_specs=[vmem] * 3,
        out_specs=(pl.BlockSpec(memory_space=pltpu.VMEM), vmem),
        scratch_shapes=[
            pltpu.VMEM((9, 1024, 128), BF16),
            pltpu.VMEM((9, 128, 1024), BF16),
            pltpu.VMEM((2, 4, 1, 128), jnp.int32),
            pltpu.VMEM((2 * EX, 1024, 1024), BF16),
            pltpu.VMEM((4, 256, 1024), F32),
            pltpu.VMEM((4, 256, 1024), F32),
            pltpu.VMEM((4, 128, 1024), BF16),
            pltpu.VMEM((2 * EX, 128), F32),
            pltpu.VMEM((3, 8, 128), F32),
            pltpu.VMEM((3, 3, 8, 128), F32),
            pltpu.VMEM((3, 2 * EX, 128), F32),
            pltpu.VMEM((3, 3, 2 * EX, 128), F32),
            pltpu.SMEM((2 * EX,), jnp.int32),
            dma((4,)),
            dma((8,)), dma((8,)),
            dma((8,)), dma((8,)),
            dma((1,)), dma((1,)),
            dma((4,)), dma((4,)),
            dma((9,)), dma((9,)),
            dma((8,)), dma((8,)),
            dma((8,)), dma((8,)),
            dma((9,)), dma((9,)),
        ],
        compiler_params=pltpu.CompilerParams(
            collective_id=2, has_side_effects=True, vmem_limit_bytes=60 * 2**20),
        cost_estimate=pl.CostEstimate(flops=2 * 10**10, bytes_accessed=10**7, transcendentals=0),
        name="score",
    )(x_mine, y_mine, ids)


def per_device(activations, out_grads, query_acts, query_grads, eig_in, eig_out, example_ids):
    x_mine, y_mine = rotate(activations, out_grads, query_acts, query_grads, eig_in, eig_out)
    corr, sums = score(x_mine, y_mine, example_ids.reshape(4, 1, 128))
    h = lax.axis_index("dp") // 2
    mine = lax.dynamic_slice_in_dim(sums, EX * h, EX, 0)
    norm_factor = 1.0 / jnp.sqrt(jnp.float32(D_IN) * jnp.float32(D_OUT))
    scores = jnp.sum(mine.reshape(EX, NQ, QTOK), axis=2).T * norm_factor
    return corr.astype(F32), scores


def solution(mesh):
    return jax.shard_map(
        per_device,
        mesh=mesh,
        in_specs=(
            P("dp", "fsdp"),
            P("dp", "fsdp"),
            P(None, "fsdp"),
            P(None, "fsdp"),
            P("fsdp", None),
            P("fsdp", None),
            P("dp", None),
        ),
        out_specs=(P("fsdp", None), P(None, "dp")),
        check_vma=False,
    )
```

time: 1110 us -> 266 us (0.24)
  waiting for transfers between devices: 728 us -> 0 us
  Pallas kernels: 0 us -> 247 us
  blocking collectives: 235 us -> 0 us
  matrix products: 61.6 us -> 0 us
  local copies, waits for them, and re-layouts: 47.5 us -> 10.8 us
  other arithmetic: 20.8 us -> 6.63 us
  between operations: 14.5 us -> 0.7 us
    all_gather x2 -> x0, waiting for transfers between devices: 367 us -> none  [the longest x1 194 us: per_device(): lax.all_gather(rows_out, 'fsdp', axis=1, tiled=True)]
    pallas_call x0 -> x2, Pallas kernels: none -> 247 us  [the longest x1 147 us: score(): pl.pallas_call(score_kernel, out_shape=(jax.ShapeDtypeStruct((256, D_OUT)...]
    psum x2 -> x0, blocking collectives: 235 us -> none  [the longest x1 152 us: per_device(): scores = lax.psum(per_query.T * norm_factor, 'fsdp')]
    reduce_scatter x1 -> x0, waiting for transfers between devices: 203 us -> none  [per_device(): lax.psum_scatter(lax.dot_general(eig_in, rows_in, (((0,), (1,)), ((), ())...]
    psum x1 -> x0, waiting for transfers between devices: 157 us -> none  [per_device(): summed = lax.psum(squares, 'dp')]
    dot_general x4 -> x0, matrix products: 61.6 us -> none  [the longest x1 24.9 us: per_device(): jnp.einsum('kem,emi->eki', in_cols, out_rows, preferred_element_type=f32)]
    gather x4 -> x0, local copies, waits for them, and re-layouts: 46.2 us -> none  [the longest x1 33.2 us: per_device(): out_rows = rot_out[row_index]]
    add x1 -> x0, other arithmetic: 11.4 us -> none  [per_device(): precond = (wide / (corrections + damping)[None]).astype(jnp.bfloat16)]
  transfers between devices with their start and end apart: 4 -> 0, of which waited for: 4 -> 0; matrix products, arithmetic and copies ran while one was open for 5% -> 0% of each run, Pallas kernels for 0% -> 0%
where the time goes in v1:
time: 266 us; the launch traced here: 265 us
  Pallas kernels  247 us (93%)
  local copies, waits for them, and re-layouts  10.8 us (4%)
  other arithmetic  6.63 us (2%)
    pallas_call x1, Pallas kernels, score(): pl.pallas_call(score_kernel, out_shape=(jax.ShapeDtypeStruct((256, D_OUT)...  147 us
    pallas_call x1, Pallas kernels, rotate(): pl.pallas_call(rotate_kernel, out_shape=(jax.ShapeDtypeStruct((9, 128, 12...  100 us
    unnamed x17, local copies, waits for them, and re-layouts  10 us
    convert_element_type x1, other arithmetic, per_device(): return (corr.astype(F32), scores)  6.58 us

profile of v1, /device:TPU:0, one launch (start us, length us, event | category | flops | bytes accessed | tf_op | source)
XLA Modules:
  0.0 265.4 jit_solution(5744426175690889526)
XLA Ops:
  0.6 0.0 copy-start
  0.7 2.2 copy-done
  2.8 0.0 copy-start.1
  2.8 2.2 copy-done.1
  5.0 0.0 copy-start.2
  5.0 0.9 copy-done.2
  6.0 0.0 copy-start.3
  6.0 0.9 copy-done.3
  6.9 0.0 copy-start.4
  6.9 0.8 copy-done.4
  7.8 0.0 copy-start.5
  7.8 0.8 copy-done.5
  8.6 100.1 %rotate.1 = (bf16[9,128,128]{2,1,0:T(8,128)(2,1)S(1)}, bf16[9,128,128]{2,1,0:T(8,128)(2,1)S(1)}) custom-call(bf16[512,256]{1,0:T(8,128)(2,1)S(1)} %copy-done.2, bf16[512,256]{1,0:T(8,128)(2,1)S(1)} %copy-done.3, bf16[128,256]{1,0:T(8,128)(2,1)S(1)} %copy-done.4, bf16[128,256]{1,0:T(8,128)(2,1)S(1)} %copy-done.5, bf16[256,8192]{1,0:T(8,128)(2,1)S(1)} %copy-done, ...), custom_call_target="tpu_custom_call" | custom-call | flops 5000000000 | bytes 10000000 | tf_op jit(solution)/shard_map/rotate/pallas_call | solution.py:234
  108.7 0.0 copy-start.6
  108.7 0.7 copy-done.6
  109.4 0.0 copy-start.7
  109.4 0.7 copy-done.7
  110.1 147.2 %score.1 = (bf16[256,8192]{1,0:T(8,128)(2,1)}, f32[16,128]{1,0:T(8,128)}) custom-call(bf16[9,128,128]{2,1,0:T(8,128)(2,1)} %copy-done.6, bf16[9,128,128]{2,1,0:T(8,128)(2,1)} %copy-done.7, s32[4,1,128]{2,1,0:T(1,128)} %bitcast.5), custom_call_target="tpu_custom_call" | custom-call | flops 20000000000 | bytes 10000000 | tf_op jit(solution)/shard_map/score/pallas_call | solution.py:513
  257.3 0.7 constant_dynamic-slice_fusion
  258.0 0.1 copy.10
  258.2 0.7 copy.11
  258.8 6.6 %convert_element_type.3 = f32[256,8192]{1,0:T(8,128)} convert(bf16[256,8192]{1,0:T(8,128)(2,1)} %get-tuple-element.8) | non-fusion elementwise | flops 2097152 | bytes 12582912 | tf_op jit(solution)/shard_map/convert_element_type | solution.py:556
  (2 shorter events, 0.0 us)
Async XLA Ops:
  0.6 2.2 copy-start
  2.8 2.2 copy-start.1
  5.0 0.9 copy-start.2
  6.0 0.9 copy-start.3
  6.9 0.8 copy-start.4
  7.8 0.8 copy-start.5
  108.7 0.7 copy-start.6
  109.4 0.7 copy-start.7

commit v2 on v1

--- a/solution.py
+++ b/solution.py
@@ -76,8 +76,10 @@
         copy.start()
     own = []
     for p in range(4):
-        own.append(pltpu.make_async_copy(
-            eig_in.at[:, pl.ds(256 * (16 * h + 4 * p + z), 256)], u_buf.at[z, p], loc.at[4 + p]))
+        for q in range(2):
+            own.append(pltpu.make_async_copy(
+                eig_in.at[:, pl.ds(256 * (16 * q + 4 * p + z) + 128 * h, 128)],
+                u_buf.at[z, p, :, pl.ds(128 * q, 128)], loc.at[12 + 2 * p + q]))
         own.append(pltpu.make_async_copy(
             eig_out.at[pl.ds(128 * h, 128), pl.ds(256 * (16 * y + 4 * p + z), 256)],
             v_buf.at[z, p, pl.ds(128 * y, 128)], loc.at[8 + p]))
@@ -92,11 +94,11 @@
         g1.append(go(remote(g_buf.at[x, mine], g_buf.at[x, mine], (gg_s, gg_r), d, device(h, c, y, xs[d], z))))
     u1, v1 = [], []
     for d in (1, 3, 2):
-        for p in range(2):
-            piece = 2 * c + p
+        for p in range(4):
             u1.append(go(remote(
-                eig_in.at[:, pl.ds(256 * (16 * h + 4 * piece + zs[d]), 256)], u_buf.at[z, piece],
-                (u_s, u_r), 2 * d + p, device(h, c, y, x, zs[d]))))
+                eig_in.at[:, pl.ds(256 * (16 * c + 4 * p + zs[d]) + 128 * h, 128)],
+                u_buf.at[z, p, :, pl.ds(128 * c, 128)],
+                (u_s, u_r), 4 * d + p, device(h, c, y, x, zs[d]))))
     for dy, yd in ((0, y), (1, oy)):
         for d in (1, 3, 2, 0):
             if dy == 0 and d == 0:
@@ -116,9 +118,9 @@
     handed = []
     for n, d in enumerate((1, 3, 2)):
         src = lax.rem(z + 4 - d, 4)
-        for p in range(2):
-            u1[2 * n + p].wait_recv()
-        part = u_buf.at[src, pl.ds(2 * c, 2)]
+        for p in range(4):
+            u1[4 * n + p].wait_recv()
+        part = u_buf.at[src, :, :, pl.ds(128 * c, 128)]
         handed.append(go(remote(part, part, (us_s, us_r), d, sibling)))
     for copy in own:
         copy.wait()
@@ -251,11 +253,11 @@
             pltpu.VMEM((ROWS, 128), BF16),
             pltpu.VMEM((ROWS, 256), F32),
             pltpu.VMEM((ROWS, 256), F32),
-            dma((12,)),
+            dma((20,)),
             dma((2,)), dma((2,)),
             dma((8,)), dma((8,)),
             dma((8,)), dma((8,)),
-            dma((8,)), dma((8,)),
+            dma((16,)), dma((16,)),
             dma((16,)), dma((16,)),
             dma((4,)), dma((4,)),
             dma((8,)), dma((8,)),
@@ -264,7 +266,7 @@
             dma((2,)), dma((2,)),
         ],
         compiler_params=pltpu.CompilerParams(
-            collective_id=1, has_side_effects=True, vmem_limit_bytes=40 * 2**20),
+            collective_id=1, has_side_effects=True, vmem_limit_bytes=60 * 2**20),
         cost_estimate=pl.CostEstimate(flops=5 * 10**9, bytes_accessed=10**7, transcendentals=0),
         name="rotate",
     )(act, grd, qa, qg, eig_in, eig_out)
@@ -279,19 +281,16 @@
     oh, oc, oy = 1 - h, 1 - c, 1 - y
     yy = 2 * h + y
     xs = [lax.rem(x + d, 4) for d in range(4)]
+    xb = [lax.rem(x + 4 - d, 4) for d in range(4)]
     zs = [lax.rem(z + d, 4) for d in range(4)]
     ys = [lax.rem(yy + d, 4) for d in range(4)]
     sibling = device(h, oc, y, x, z)
-
-    def at_y(v):
-        return device(v // 2, c, lax.rem(v, 2), x, z)
-
-    plane = []
-    for dy in range(4):
-        for dx in range(4):
-            if dy or dx:
-                plane.append(device(ys[dy] // 2, c, lax.rem(ys[dy], 2), xs[dx], z))
-    greet([sibling] + plane + [device(h, c, y, x, zs[d]) for d in (1, 2, 3)])
+    greet(
+        [sibling, device(h, c, oy, x, z), device(oh, c, oy, x, z)]
+        + [device(h, c, y, xs[d], z) for d in (1, 2, 3)]
+        + [device(oh, c, y, xs[d], z) for d in (0, 1, 2, 3)]
+        + [device(h, c, y, x, zs[d]) for d in (1, 2, 3)]
+    )
     started = []
 
     def go(copy):
@@ -299,33 +298,33 @@
         started.append(copy)
         return copy
 
-    def x_slot(xv, yv):
-        return x_all.at[:, pl.ds(pl.multiple_of(128 * (2 * xv + yv), 128), 128), :]
-
-    def y_slot(zv, hv):
-        return y_all.at[:, :, pl.ds(pl.multiple_of(128 * (2 * zv + hv), 128), 128)]
+    def x_slot(xv, hv):
+        return x_all.at[:, pl.ds(pl.multiple_of(128 * (2 * xv + hv), 128), 128), :]
+
+    def y_slot(zv, yv):
+        return y_all.at[:, :, pl.ds(pl.multiple_of(128 * (2 * zv + yv), 128), 128)]
 
     across_h, across_y = device(oh, c, y, x, z), device(h, c, oy, x, z)
     ids_copy = go(remote(ids, id_all.at[h], (id_s, id_r), 0, across_h))
-    xy = go(remote(x_mine, x_slot(x, y), (gx_s, gx_r), 0, across_y))
-    yh = go(remote(y_mine, y_slot(z, h), (gy_s, gy_r), 0, across_h))
+    xh = go(remote(x_mine, x_slot(x, h), (gx_s, gx_r), 0, across_h))
+    yy_copy = go(remote(y_mine, y_slot(z, y), (gy_s, gy_r), 0, across_y))
     got = []
     for d in (1, 3, 2):
-        got.append(go(remote(x_mine, x_slot(x, y), (gx_s, gx_r), d, device(h, c, y, xs[d], z))))
-        got.append(go(remote(y_mine, y_slot(z, h), (gy_s, gy_r), d, device(h, c, y, x, zs[d]))))
+        got.append(go(remote(x_mine, x_slot(x, h), (gx_s, gx_r), d, device(h, c, y, xs[d], z))))
+        got.append(go(remote(y_mine, y_slot(z, y), (gy_s, gy_r), d, device(h, c, y, x, zs[d]))))
     local = [
-        pltpu.make_async_copy(x_mine, x_slot(x, y), loc.at[0]),
-        pltpu.make_async_copy(y_mine, y_slot(z, h), loc.at[1]),
+        pltpu.make_async_copy(x_mine, x_slot(x, h), loc.at[0]),
+        pltpu.make_async_copy(y_mine, y_slot(z, y), loc.at[1]),
         pltpu.make_async_copy(ids, id_all.at[h], loc.at[2]),
     ]
     for copy in local:
         copy.start()
-    xy.wait_recv()
+    xh.wait_recv()
     for d in (1, 3, 2):
-        got.append(go(remote(x_slot(x, oy), x_slot(x, oy), (gx_s, gx_r), 4 + d, device(h, c, y, xs[d], z))))
-    yh.wait_recv()
+        got.append(go(remote(x_slot(x, oh), x_slot(x, oh), (gx_s, gx_r), 4 + d, device(h, c, y, xs[d], z))))
+    yy_copy.wait_recv()
     for d in (1, 3, 2):
-        got.append(go(remote(y_slot(z, oh), y_slot(z, oh), (gy_s, gy_r), 4 + d, device(h, c, y, x, zs[d]))))
+        got.append(go(remote(y_slot(z, oy), y_slot(z, oy), (gy_s, gy_r), 4 + d, device(h, c, y, x, zs[d]))))
     for copy in local:
         copy.wait()
     ids_copy.wait_recv()
@@ -334,47 +333,45 @@
         for e in range(EX):
             first = jnp.sum((row < e).astype(jnp.int32))
             blks[8 * g + e] = jnp.minimum(first // 128, 2)
+    sq[...] = jnp.zeros_like(sq)
+    acc[...] = jnp.zeros_like(acc)
     for copy in got:
         copy.wait_recv()
 
-    def quarter(kt, _):
+    def quarter(kt):
         rows = pl.ds(pl.multiple_of(256 * kt, 256), 256)
 
-        def pair(n, _):
-            g, e = n // 8, lax.rem(n, 8)
-            blk = blks[n]
-            parts = []
-            for b in range(2):
-                keep = id_all[g, blk + b] == e
-                parts.append(jnp.where(keep, x_all[4 * g + blk + b, rows, :].astype(F32), 0.0).astype(BF16))
-            left = jnp.concatenate(parts, axis=1)
-            for it in range(2):
-                cols = pl.ds(512 * it, 512)
-                right = jnp.concatenate(
-                    [y_all[4 * g + blk, :, cols], y_all[4 * g + blk + 1, :, cols]], axis=0)
-                value = jnp.dot(left, right, preferred_element_type=F32).astype(BF16)
-                rot[n, rows, cols] = value
-                wide = value.astype(F32)
-
-                @pl.when(n == 0)
-                def _():
-                    sq[kt, :, cols] = wide * wide
-
-                @pl.when(n > 0)
-                def _():
-                    sq[kt, :, cols] += wide * wide
-            return 0
-
-        lax.fori_loop(0, 2 * EX, pair, 0)
-        copy = remote(sq.at[kt], sq_got.at[kt], (sq_s, sq_r), kt, sibling)
-        copy.start()
-        return 0
-
-    lax.fori_loop(0, 4, quarter, 0)
+        def pairs(m, _):
+            lefts, blocks = [], []
+            for u in range(4):
+                n = 4 * m + u
+                g, e = n // 8, lax.rem(n, 8)
+                blk = blks[n]
+                parts = []
+                for b in range(2):
+                    keep = id_all[g, blk + b] == e
+                    parts.append(jnp.where(keep, x_all[4 * g + blk + b, rows, :].astype(F32), 0.0).astype(BF16))
+                lefts.append(jnp.concatenate(parts, axis=1))
+                blocks.append(4 * g + blk)
+            for it in range(4):
+                cols = pl.ds(256 * it, 256)
+                total = sq[kt, :, cols]
+                for u in range(4):
+                    right = jnp.concatenate([y_all[blocks[u], :, cols], y_all[blocks[u] + 1, :, cols]], axis=0)
+                    value = jnp.dot(lefts[u], right, preferred_element_type=F32).astype(BF16)
+                    rot[4 * m + u, rows, cols] = value
+                    wide = value.astype(F32)
+                    total = total + wide * wide
+                sq[kt, :, cols] = total
+            return 0
+
+        lax.fori_loop(0, EX // 2, pairs, 0)
+
+    def sq_copy(kt):
+        return remote(sq.at[kt], sq_got.at[kt], (sq_s, sq_r), kt, sibling)
 
     def add_up(kt, total):
-        copy = remote(sq.at[kt], sq_got.at[kt], (sq_s, sq_r), kt, sibling)
-        copy.wait()
+        sq_copy(kt).wait()
 
         def chunk(i, total):
             part = pl.ds(pl.multiple_of(32 * i, 32), 32)
@@ -389,7 +386,31 @@
         c_stage[kt] = sq[kt, pl.ds(pl.multiple_of(128 * c, 128), 128), :].astype(BF16)
         return total
 
-    total = lax.fori_loop(0, 4, add_up, jnp.zeros((8, 128), F32))
+    def slab(xv, hv):
+        return corr.at[2 * xv + hv, pl.ds(pl.multiple_of(128 * c, 128), 128), :]
+
+    def out_copies(j):
+        copies = []
+        for hd in range(2):
+            if hd or j:
+                copies.append(pltpu.make_async_remote_copy(
+                    src_ref=c_stage.at[xs[j]], dst_ref=slab(x, h), send_sem=o_s.at[4 * hd + j],
+                    recv_sem=o_r.at[4 * hd + j], device_id=device((h, oh)[hd], c, y, xs[j], z),
+                    device_id_type=MESH))
+        return copies
+
+    own_out = pltpu.make_async_copy(c_stage.at[x], slab(x, h), loc.at[3])
+    total = jnp.zeros((8, 128), F32)
+    for j in range(4):
+        quarter(xs[j])
+        sq_copy(xs[j]).start()
+        if j:
+            total = add_up(xs[j - 1], total)
+            for copy in out_copies(j - 1):
+                copy.start()
+            if j == 1:
+                own_out.start()
+    total = add_up(xs[3], total)
 
     def spread(value, n, buf, got_buf, sems, where):
         buf[n] = value
@@ -397,6 +418,9 @@
         for copy in copies:
             copy.wait_recv()
         return buf[n] + got_buf[n, 0] + got_buf[n, 1] + got_buf[n, 2]
+
+    def at_y(v):
+        return device(v // 2, c, lax.rem(v, 2), x, z)
 
     steps = (
         lambda d: device(h, c, y, x, zs[d]),
@@ -406,43 +430,10 @@
     for n in range(3):
         total = spread(total, n, red, red_got, (t_s, t_r), steps[n])
     damping = 0.5 * (jnp.sum(total) / (float(D_IN) * float(D_OUT)))
-
-    def slab(yv, xv):
-        return corr.at[pl.ds(pl.multiple_of(128 * c, 128), 128),
-                       pl.ds(pl.multiple_of(1024 * (4 * yv + xv), 1024), 1024)]
-
-    me = 4 * y + x
-
-    def is_me(hv, xv):
-        return jnp.logical_and(jnp.logical_and(hv == h, h == y), xv == x)
-
-    def hand_out(start):
-        for hd in range(2):
-            for d in range(4):
-                hv, xv = (h, oh)[hd], xs[d]
-                slot = 4 * hd + d
-                copy = pltpu.make_async_remote_copy(
-                    src_ref=c_stage.at[xv], dst_ref=slab(y, x), send_sem=o_s.at[slot], recv_sem=o_r.at[me],
-                    device_id=device(hv, c, h, xv, z), device_id_type=MESH)
-                run = copy.start if start else copy.wait_send
-                if hd == 0 and d == 0:
-                    @pl.when(h != y)
-                    def _():
-                        run()
-
-                    @pl.when(h == y)
-                    def _():
-                        own = pltpu.make_async_copy(c_stage.at[x], slab(y, x), loc.at[3])
-                        if start:
-                            own.start()
-                        else:
-                            own.wait()
-                else:
-                    run()
-
-    hand_out(True)
-
-    def second(kt, _):
+    for copy in out_copies(3):
+        copy.start()
+
+    def second(kt):
         rows = pl.ds(pl.multiple_of(256 * kt, 256), 256)
 
         def invert(i, _):
@@ -451,58 +442,43 @@
             return 0
 
         lax.fori_loop(0, 8, invert, 0)
-        query_in = x_all[8, rows, :].astype(F32)
-
-        def pair(n, _):
-            cond = (rot[n, rows, :].astype(F32) * sq[kt]).astype(BF16)
-            part = lax.dot_general(
-                cond, y_all[8], (((1,), (1,)), ((), ())), preferred_element_type=F32)
-            weighted = part * query_in
-            value = jnp.sum(weighted, axis=0, keepdims=True)
-
-            @pl.when(kt == 0)
-            def _():
-                acc[pl.ds(n, 1), :] = value
-
-            @pl.when(kt > 0)
-            def _():
-                acc[pl.ds(n, 1), :] += value
-            return 0
-
-        lax.fori_loop(0, 2 * EX, pair, 0)
-        return 0
-
-    lax.fori_loop(0, 4, second, 0)
-    hand_out(False)
-
-    def forward(i, _):
-        yv, xv = i // 4, lax.rem(i, 4)
-        mine = jnp.logical_and(h == y, i == me)
-
-        @pl.when(jnp.logical_not(mine))
-        def _():
-            pltpu.make_async_remote_copy(
-                src_ref=c_stage.at[0], dst_ref=slab(yv, xv), send_sem=o_s.at[0], recv_sem=o_r.at[i],
-                device_id=sibling, device_id_type=MESH).wait_recv()
-        pltpu.make_async_remote_copy(
-            src_ref=slab(yv, xv), dst_ref=slab(yv, xv), send_sem=f_s.at[i], recv_sem=f_r.at[i],
-            device_id=sibling, device_id_type=MESH).start()
-        return 0
-
-    lax.fori_loop(0, 8, forward, 0)
+
+        def pairs(m, _):
+            query_in = x_all[8, rows, :].astype(F32)
+            sums = [None] * 4
+            for it in range(4):
+                cols = pl.ds(256 * it, 256)
+                factor = sq[kt, :, cols]
+                query_out = y_all[8, :, cols]
+                for u in range(4):
+                    cond = (rot[4 * m + u, rows, cols].astype(F32) * factor).astype(BF16)
+                    part = lax.dot_general(
+                        cond, query_out, (((1,), (1,)), ((), ())), preferred_element_type=F32)
+                    sums[u] = part if it == 0 else sums[u] + part
+            for u in range(4):
+                acc[pl.ds(4 * m + u, 1), :] += jnp.sum(sums[u] * query_in, axis=0, keepdims=True)
+            return 0
+
+        lax.fori_loop(0, EX // 2, pairs, 0)
+
+    def hand_on(xv, hv):
+        return remote(slab(xv, hv), slab(xv, hv), (f_s, f_r), 2 * xv + hv, sibling)
+
+    for j in range(4):
+        second(xs[j])
+        for copy in out_copies(j):
+            copy.wait()
+        if j == 0:
+            own_out.wait()
+        for hv in (h, oh):
+            hand_on(xb[j], hv).start()
     value = acc[...]
     for n in range(3):
         value = spread(value, n, red2, red2_got, (p_s, p_r), steps[n])
     scores[...] = value
-
-    def last(i, _):
-        yv, xv = i // 4, lax.rem(i, 4)
-        pltpu.make_async_remote_copy(
-            src_ref=slab(yv, xv), dst_ref=slab(yv, xv), send_sem=f_s.at[i], recv_sem=f_r.at[i],
-            device_id=sibling, device_id_type=MESH).wait()
-        return 0
-
-    lax.fori_loop(0, 8, last, 0)
+    for j in range(4):
+        for hv in (h, oh):
+            hand_on(xb[j], hv).wait()
     for copy in started:
         copy.wait_send()
 
@@ -512,7 +488,7 @@
     vmem = pl.BlockSpec(memory_space=pltpu.VMEM)
     return pl.pallas_call(
         score_kernel,
-        out_shape=(jax.ShapeDtypeStruct((256, D_OUT), BF16), jax.ShapeDtypeStruct((2 * EX, 128), F32)),
+        out_shape=(jax.ShapeDtypeStruct((8, 256, 1024), BF16), jax.ShapeDtypeStruct((2 * EX, 128), F32)),
         in_specs=[vmem] * 3,
         out_specs=(pl.BlockSpec(memory_space=pltpu.VMEM), vmem),
         scratch_shapes=[
@@ -546,6 +522,36 @@
     )(x_mine, y_mine, ids)
 
 
+def widen_kernel(corr, out, stage, sems):
+    def copy(n):
+        yv, xv = n // 4, n % 4
+        return pltpu.make_async_copy(stage.at[n % 2], out.at[:, pl.ds(1024 * (4 * yv + xv), 1024)], sems.at[n % 2])
+
+    for n in range(8):
+        yv, xv = n // 4, n % 4
+        if n >= 2:
+            copy(n - 2).wait()
+        for zv in range(4):
+            for hv in range(2):
+                stage[n % 2, :, pl.ds(128 * (2 * zv + hv), 128)] = corr[
+                    2 * xv + hv, :, pl.ds(128 * (2 * zv + yv), 128)].astype(F32)
+        copy(n).start()
+    copy(6).wait()
+    copy(7).wait()
+
+
+def widen(corr):
+    return pl.pallas_call(
+        widen_kernel,
+        out_shape=jax.ShapeDtypeStruct((256, D_OUT), F32),
+        in_specs=[pl.BlockSpec(memory_space=pltpu.VMEM)],
+        out_specs=pl.BlockSpec(memory_space=pl.ANY),
+        scratch_shapes=[pltpu.VMEM((2, 256, 1024), F32), pltpu.SemaphoreType.DMA((2,))],
+        compiler_params=pltpu.CompilerParams(vmem_limit_bytes=60 * 2**20),
+        name="widen",
+    )(corr)
+
+
 def per_device(activations, out_grads, query_acts, query_grads, eig_in, eig_out, example_ids):
     x_mine, y_mine = rotate(activations, out_grads, query_acts, query_grads, eig_in, eig_out)
     corr, sums = score(x_mine, y_mine, example_ids.reshape(4, 1, 128))
@@ -553,7 +559,7 @@
     mine = lax.dynamic_slice_in_dim(sums, EX * h, EX, 0)
     norm_factor = 1.0 / jnp.sqrt(jnp.float32(D_IN) * jnp.float32(D_OUT))
     scores = jnp.sum(mine.reshape(EX, NQ, QTOK), axis=2).T * norm_factor
-    return corr.astype(F32), scores
+    return widen(corr), scores
 
 
 def solution(mesh):

time: 266 us -> 213 us (0.80)
  Pallas kernels: 247 us -> 211 us
  local copies, waits for them, and re-layouts: 10.8 us -> 1.45 us
  other arithmetic: 6.63 us -> 0.05 us
    pallas_call x1 -> x2, Pallas kernels: 147 us -> 109 us  [the longest x1 102 us: score(): pl.pallas_call(score_kernel, out_shape=(jax.ShapeDtypeStruct((8, 256, 102...]
    unnamed x17 -> x1, local copies, waits for them, and re-layouts: 10 us -> 0.66 us
    convert_element_type x1 -> x0, other arithmetic: 6.58 us -> none  [per_device(): return (corr.astype(F32), scores)]
where the time goes in v2:
time: 213 us
  Pallas kernels  211 us (99%)
    pallas_call x1, Pallas kernels, score(): pl.pallas_call(score_kernel, out_shape=(jax.ShapeDtypeStruct((8, 256, 102...  102 us
    pallas_call x1, Pallas kernels, rotate(): pl.pallas_call(rotate_kernel, out_shape=(jax.ShapeDtypeStruct((9, 128, 12...  102 us
    pallas_call x1, Pallas kernels, widen(): pl.pallas_call(widen_kernel, out_shape=jax.ShapeDtypeStruct((256, D_OUT),...  6.9 us

profile of v2, /device:TPU:0, one launch (start us, length us, event | category | flops | bytes accessed | tf_op | source)
XLA Modules:
  0.0 213.0 jit_solution(6083570378578843188)
XLA Ops:
  0.6 101.9 %rotate.1 = (bf16[9,128,128]{2,1,0:T(8,128)(2,1)}, bf16[9,128,128]{2,1,0:T(8,128)(2,1)}) custom-call(bf16[512,256]{1,0:T(8,128)(2,1)} %act.1, bf16[512,256]{1,0:T(8,128)(2,1)} %grd.1, bf16[128,256]{1,0:T(8,128)(2,1)} %qa.1, bf16[128,256]{1,0:T(8,128)(2,1)} %qg.1, bf16[256,8192]{1,0:T(8,128)(2,1)} %eig_in.1, bf16[256,8192]{1,0:T(8,128)(2,1)} %eig_out.1), custom_call_target="tpu_custom_call" | custom-call | flops 5000000000 | bytes 10000000 | tf_op jit(solution)/shard_map/rotate/pallas_call | solution.py:236
  102.6 102.0 %score.1 = (bf16[8,256,1024]{2,1,0:T(8,128)(2,1)}, f32[16,128]{1,0:T(8,128)}) custom-call(bf16[9,128,128]{2,1,0:T(8,128)(2,1)} %get-tuple-element.6.x_mine, bf16[9,128,128]{2,1,0:T(8,128)(2,1)} %get-tuple-element.7.y_mine, s32[4,1,128]{2,1,0:T(1,128)} %bitcast.5), custom_call_target="tpu_custom_call" | custom-call | flops 20000000000 | bytes 10000000 | tf_op jit(solution)/shard_map/score/pallas_call | solution.py:489
  204.6 0.7 constant_dynamic-slice_fusion
  205.3 0.1 copy.10
  205.5 0.7 copy.11
  206.1 6.9 %widen.1 = f32[256,8192]{1,0:T(8,128)} custom-call(bf16[8,256,1024]{2,1,0:T(8,128)(2,1)} %get-tuple-element.8.corr), custom_call_target="tpu_custom_call" | custom-call | tf_op jit(solution)/shard_map/widen/pallas_call | solution.py:544
  (2 shorter events, 0.0 us)

commit v3 on v2

v3 whole, which is shorter than its diff:
```python
import jax
import jax.numpy as jnp
from jax import lax
from jax.experimental import pallas as pl
from jax.experimental.pallas import tpu as pltpu
from jax.sharding import PartitionSpec as P

D_IN = 8192
D_OUT = 8192
EX = 8
NQ = 32
QTOK = 4
ROWS = 1152
MESH = pl.DeviceIdType.MESH
F32 = jnp.float32
BF16 = jnp.bfloat16


def place():
    dp, fs = lax.axis_index("dp"), lax.axis_index("fsdp")
    return dp // 2, lax.rem(dp, 2), fs // 16, lax.rem(fs // 4, 4), lax.rem(fs, 4)


def device(h, c, y, x, z):
    return (2 * h + c, 16 * y + 4 * x + z)


def greet(partners):
    barrier = pltpu.get_barrier_semaphore()
    for partner in partners:
        pl.semaphore_signal(barrier, 1, device_id=partner, device_id_type=MESH)
    pl.semaphore_wait(barrier, len(partners))


def remote(src, dst, sems, slot, target):
    return pltpu.make_async_remote_copy(
        src_ref=src, dst_ref=dst, send_sem=sems[0].at[slot], recv_sem=sems[1].at[slot],
        device_id=target, device_id_type=MESH,
    )


def rotate_kernel(
    act, grd, qa, qg, eig_in, eig_out, x_out, y_out,
    a_buf, g_buf, u_buf, v_buf, in_bufs, out_bufs,
    loc, h_s, h_r, ag_s, ag_r, gg_s, gg_r, u_s, u_r, v_s, v_r, us_s, us_r, vsib_s, vsib_r,
    in_sems, out_sems,
):
    h, c, y, x, z = place()
    oh, oc, oy = 1 - h, 1 - c, 1 - y
    xs = [lax.rem(x + d, 4) for d in range(4)]
    zs = [lax.rem(z + d, 4) for d in range(4)]
    sibling = device(h, oc, y, x, z)
    partner = device(h, c, oy, x, z)
    greet(
        [sibling, device(oh, c, y, x, z), partner]
        + [device(h, c, y, xs[d], z) for d in (1, 2, 3)]
        + [device(h, c, y, x, zs[d]) for d in (1, 2, 3)]
        + [device(h, c, oy, x, zs[d]) for d in (1, 2, 3)]
    )
    started = []

    def go(copy):
        copy.start()
        started.append(copy)
        return copy

    ah = go(remote(act, a_buf.at[z, pl.ds(640, 512)], (h_s, h_r), 0, device(oh, c, y, x, z)))
    gh = go(remote(grd, g_buf.at[x, pl.ds(640, 512)], (h_s, h_r), 1, device(oh, c, y, x, z)))
    local = [
        pltpu.make_async_copy(act, a_buf.at[z, pl.ds(0, 512)], loc.at[0]),
        pltpu.make_async_copy(qa, a_buf.at[z, pl.ds(512, 128)], loc.at[1]),
        pltpu.make_async_copy(grd, g_buf.at[x, pl.ds(0, 512)], loc.at[2]),
        pltpu.make_async_copy(qg, g_buf.at[x, pl.ds(512, 128)], loc.at[3]),
    ]
    for copy in local:
        copy.start()
    u1 = []
    for d in (1, 3, 2):
        for p in range(4):
            u1.append(go(remote(
                eig_in.at[:, pl.ds(256 * (16 * c + 4 * p + zs[d]) + 128 * h, 128)],
                u_buf.at[z, p, :, pl.ds(128 * c, 128)],
                (u_s, u_r), 4 * d + p, device(h, c, y, x, zs[d]))))
    for copy in local:
        copy.wait()
    mine, other = pl.ds(0, 640), pl.ds(640, 512)
    a1, g1, a2, g2 = [], [], [], []
    for d in (1, 3, 2):
        a1.append(go(remote(a_buf.at[z, mine], a_buf.at[z, mine], (ag_s, ag_r), d, device(h, c, y, x, zs[d]))))
        g1.append(go(remote(g_buf.at[x, mine], g_buf.at[x, mine], (gg_s, gg_r), d, device(h, c, y, xs[d], z))))
    own = []
    for p in range(4):
        for q in range(2):
            own.append(pltpu.make_async_copy(
                eig_in.at[:, pl.ds(256 * (16 * q + 4 * p + z) + 128 * h, 128)],
                u_buf.at[z, p, :, pl.ds(128 * q, 128)], loc.at[12 + 2 * p + q]))
        own.append(pltpu.make_async_copy(
            eig_out.at[pl.ds(128 * h, 128), pl.ds(256 * (16 * y + 4 * p + z), 256)],
            v_buf.at[z, p, pl.ds(128 * y, 128)], loc.at[8 + p]))
    for copy in own:
        copy.start()
    ah.wait_recv()
    gh.wait_recv()
    for d in (1, 3, 2):
        a2.append(go(remote(a_buf.at[z, other], a_buf.at[z, other], (ag_s, ag_r), 4 + d, device(h, c, y, x, zs[d]))))
        g2.append(go(remote(g_buf.at[x, other], g_buf.at[x, other], (gg_s, gg_r), 4 + d, device(h, c, y, xs[d], z))))
    handed = []
    for n, d in enumerate((1, 3, 2)):
        src = lax.rem(z + 4 - d, 4)
        for p in range(4):
            u1[4 * n + p].wait_recv()
        part = u_buf.at[src, :, :, pl.ds(128 * c, 128)]
        handed.append(go(remote(part, part, (us_s, us_r), d, sibling)))
    for copy in own:
        copy.wait()
    for copy in a1:
        copy.wait_recv()
    v1 = []
    for dy, yd in ((1, oy), (0, y)):
        for d in (1, 3, 2, 0):
            if dy == 0 and d == 0:
                continue
            for p in range(2):
                piece = 2 * c + p
                v1.append((dy, d, p, go(remote(
                    eig_out.at[pl.ds(128 * h, 128), pl.ds(256 * (16 * yd + 4 * piece + zs[d]), 256)],
                    v_buf.at[z, piece, pl.ds(128 * y, 128)],
                    (v_s, v_r), 8 * dy + 2 * d + p, device(h, c, yd, x, zs[d])))))
    for copy in handed:
        copy.wait_recv()

    def halves(total):
        low, high = total[:, :128], total[:, 128:]
        return jnp.where(y == 0, low, high), jnp.where(y == 0, high, low)

    def rows_loop(first, count, tile, body):
        def step(i, _):
            start = pl.multiple_of(i * tile, tile)
            body(pl.ds(start, tile), pl.ds(pl.multiple_of(first + start, 64), tile))
            return 0
        lax.fori_loop(0, count // tile, step, 0)

    def side(product, bufs, sems, ring, coords):
        r_send, r_got, r_own, q_send, q_got, p_send, p_got, p_own, w_send, w_got, w_own = bufs
        r_s, r_r, w_s, w_r, y_s, y_r = sems
        sent = {}

        def ring_first():
            sent["ring"] = []
            for n, d in enumerate((1, 3, 2, 0)):
                if d:
                    def body(rows, src):
                        r_send[n, rows, :] = product(src, coords[d], 320).astype(BF16)
                    rows_loop(0, 640, 320, body)
                    sent["ring"].append(go(remote(r_send.at[n], r_got.at[n], (r_s, r_r), n, ring(d))))
                else:
                    def body(rows, src):
                        r_own[rows, :] = product(src, coords[0], 320)
                    rows_loop(0, 640, 320, body)

        def partner_first():
            for d in range(4):
                def body(rows, src):
                    keep, give = halves(product(src, coords[d], 256))
                    p_own[d, rows, :] = keep
                    p_send[coords[d], rows, :] = give.astype(BF16)
                rows_loop(640, 512, 256, body)
            sent["partner"] = go(remote(p_send, p_got, (y_s, y_r), 0, partner))

        def partner_then_ring():
            sent["partner"].wait_recv()
            sent["late"] = []
            for n, d in enumerate((1, 3, 2, 0)):
                def body(rows, _):
                    total = p_own[d, rows, :] + p_got[coords[d], rows, :].astype(F32)
                    if d:
                        w_send[n, rows, :] = total.astype(BF16)
                    else:
                        w_own[rows, :] = total
                rows_loop(0, 512, 256, body)
                if d:
                    sent["late"].append(go(remote(w_send.at[n], w_got.at[n], (w_s, w_r), n, ring(d))))

        def ring_then_partner():
            for copy in sent["ring"]:
                copy.wait_recv()

            def body(rows, _):
                total = r_own[rows, :]
                for n in range(3):
                    total += r_got[n, rows, :].astype(F32)
                r_own[rows, :] = total
                q_send[rows, :] = halves(total)[1].astype(BF16)
            rows_loop(0, 640, 128, body)
            sent["last"] = go(remote(q_send, q_got, (y_s, y_r), 1, partner))

        def finish(out, turn):
            for copy in sent["late"]:
                copy.wait_recv()

            def late(i, _):
                rows = pl.ds(pl.multiple_of(i * 128, 128), 128)
                total = w_own[rows, :]
                for n in range(3):
                    total += w_got[n, rows, :].astype(F32)
                out[4 * oh + i] = (total.T if turn else total).astype(BF16)
                return 0
            lax.fori_loop(0, 4, late, 0)
            sent["last"].wait_recv()

            def first(i, _):
                rows = pl.ds(pl.multiple_of(i * 128, 128), 128)
                total = halves(r_own[rows, :])[0] + q_got[rows, :].astype(F32)
                out[jnp.where(i < 4, 4 * h + i, 8)] = (total.T if turn else total).astype(BF16)
                return 0
            lax.fori_loop(0, 5, first, 0)

        return ring_first, partner_first, partner_then_ring, ring_then_partner, finish

    def product_in(rows, piece, tile):
        total = jnp.zeros((tile, 256), F32)
        for s in range(4):
            total += jnp.dot(a_buf[s, rows, :], u_buf[s, piece], preferred_element_type=F32)
        return total

    def product_out(rows, piece, tile):
        total = jnp.zeros((tile, 256), F32)
        for s in range(4):
            total += lax.dot_general(
                g_buf[s, rows, :], v_buf[piece, s], (((1,), (1,)), ((), ())), preferred_element_type=F32)
        return total

    in_side = side(product_in, in_bufs, in_sems, lambda d: device(h, c, y, xs[d], z), xs)
    out_side = side(product_out, out_bufs, out_sems, lambda d: device(h, c, y, x, zs[d]), zs)
    in_side[0]()
    for copy in a2:
        copy.wait_recv()
    in_side[1]()
    vhanded = []
    for n in range(len(v1) // 2):
        dy, d, _, copy = v1[2 * n]
        copy.wait_recv()
        v1[2 * n + 1][3].wait_recv()
        src = lax.rem(z + 4 - d, 4)
        part = v_buf.at[src, pl.ds(2 * c, 2), pl.ds(128 * (oy if dy else y), 128)]
        vhanded.append(go(remote(part, part, (vsib_s, vsib_r), 4 * dy + d, sibling)))
    for copy in g1 + g2 + vhanded:
        copy.wait_recv()
    out_side[1]()
    out_side[0]()
    in_side[2]()
    in_side[3]()
    out_side[2]()
    out_side[3]()
    in_side[4](x_out, True)
    out_side[4](y_out, False)
    for copy in started:
        copy.wait_send()


def rotate(act, grd, qa, qg, eig_in, eig_out):
    dma = pltpu.SemaphoreType.DMA
    any_ = pl.BlockSpec(memory_space=pl.ANY)
    vmem = pl.BlockSpec(memory_space=pltpu.VMEM)

    def side_bufs():
        return (
            pltpu.VMEM((3, 640, 256), BF16), pltpu.VMEM((3, 640, 256), BF16), pltpu.VMEM((640, 256), F32),
            pltpu.VMEM((640, 128), BF16), pltpu.VMEM((640, 128), BF16),
            pltpu.VMEM((4, 512, 128), BF16), pltpu.VMEM((4, 512, 128), BF16), pltpu.VMEM((4, 512, 128), F32),
            pltpu.VMEM((3, 512, 128), BF16), pltpu.VMEM((3, 512, 128), BF16), pltpu.VMEM((512, 128), F32),
        )

    def side_sems():
        return tuple([dma((3,))] * 4 + [dma((2,))] * 2)

    return pl.pallas_call(
        rotate_kernel,
        out_shape=(jax.ShapeDtypeStruct((9, 128, 128), BF16), jax.ShapeDtypeStruct((9, 128, 128), BF16)),
        in_specs=[any_] * 6,
        out_specs=(vmem, vmem),
        scratch_shapes=[
            pltpu.VMEM((4, ROWS, 256), BF16),
            pltpu.VMEM((4, ROWS, 256), BF16),
            pltpu.VMEM((4, 4, 256, 256), BF16),
            pltpu.VMEM((4, 4, 256, 256), BF16),
            side_bufs(), side_bufs(),
            dma((20,)),
            dma((2,)), dma((2,)),
            dma((8,)), dma((8,)),
            dma((8,)), dma((8,)),
            dma((16,)), dma((16,)),
            dma((16,)), dma((16,)),
            dma((4,)), dma((4,)),
            dma((8,)), dma((8,)),
            side_sems(), side_sems(),
        ],
        compiler_params=pltpu.CompilerParams(
            collective_id=1, has_side_effects=True, vmem_limit_bytes=60 * 2**20),
        cost_estimate=pl.CostEstimate(flops=5 * 10**9, bytes_accessed=10**7, transcendentals=0),
        name="rotate",
    )(act, grd, qa, qg, eig_in, eig_out)


def score_kernel(
    x_mine, y_mine, ids, corr, scores,
    x_all, y_all, id_all, rot, sq, sq_got, c_stage, acc, gram, red, red_got, red2, red2_got, blks,
    loc, gx_s, gx_r, gy_s, gy_r, id_s, id_r, sq_s, sq_r, t_s, t_r, o_s, o_r, f_s, f_r, p_s, p_r,
):
    h, c, y, x, z = place()
    oh, oc, oy = 1 - h, 1 - c, 1 - y
    yy = 2 * h + y
    xs = [lax.rem(x + d, 4) for d in range(4)]
    xb = [lax.rem(x + 4 - d, 4) for d in range(4)]
    zs = [lax.rem(z + d, 4) for d in range(4)]
    ys = [lax.rem(yy + d, 4) for d in range(4)]
    sibling = device(h, oc, y, x, z)
    greet(
        [sibling, device(h, c, oy, x, z), device(oh, c, oy, x, z)]
        + [device(h, c, y, xs[d], z) for d in (1, 2, 3)]
        + [device(oh, c, y, xs[d], z) for d in (0, 1, 2, 3)]
        + [device(h, c, y, x, zs[d]) for d in (1, 2, 3)]
    )
    started = []

    def go(copy):
        copy.start()
        started.append(copy)
        return copy

    groups = (pl.ds(0, 4), pl.ds(4, 5))

    def x_slot(t, xv, hv):
        return x_all[t].at[:, pl.ds(pl.multiple_of(128 * (2 * xv + hv), 128), 128), :]

    def y_slot(t, zv, yv):
        return y_all[t].at[:, :, pl.ds(pl.multiple_of(128 * (2 * zv + yv), 128), 128)]

    across_h, across_y = device(oh, c, y, x, z), device(h, c, oy, x, z)
    ids_copy = go(remote(ids, id_all.at[h], (id_s, id_r), 0, across_h))
    firsts, got = [], ([], [])
    for t in range(2):
        x_part, y_part = x_mine.at[groups[t]], y_mine.at[groups[t]]
        firsts.append((
            go(remote(x_part, x_slot(t, x, h), (gx_s, gx_r), 8 * t, across_h)),
            go(remote(y_part, y_slot(t, z, y), (gy_s, gy_r), 8 * t, across_y)),
        ))
    for t in range(2):
        x_part, y_part = x_mine.at[groups[t]], y_mine.at[groups[t]]
        for d in (1, 3, 2):
            got[t].append(go(remote(x_part, x_slot(t, x, h), (gx_s, gx_r), 8 * t + d, device(h, c, y, xs[d], z))))
            got[t].append(go(remote(y_part, y_slot(t, z, y), (gy_s, gy_r), 8 * t + d, device(h, c, y, x, zs[d]))))
        for copy in firsts[t]:
            copy.wait_recv()
        for d in (1, 3, 2):
            got[t].append(go(remote(
                x_slot(t, x, oh), x_slot(t, x, oh), (gx_s, gx_r), 8 * t + 4 + d, device(h, c, y, xs[d], z))))
            got[t].append(go(remote(
                y_slot(t, z, oy), y_slot(t, z, oy), (gy_s, gy_r), 8 * t + 4 + d, device(h, c, y, x, zs[d]))))
    local = [pltpu.make_async_copy(ids, id_all.at[h], loc.at[2])]
    for t in range(2):
        local.append(pltpu.make_async_copy(x_mine.at[groups[t]], x_slot(t, x, h), loc.at[4 * t]))
        local.append(pltpu.make_async_copy(y_mine.at[groups[t]], y_slot(t, z, y), loc.at[1 + 4 * t]))
    for copy in local:
        copy.start()
    sq[...] = jnp.zeros_like(sq)
    acc[...] = jnp.zeros_like(acc)
    for copy in local:
        copy.wait()
    ids_copy.wait_recv()
    for g in range(2):
        row = id_all[g]
        for e in range(EX):
            first = jnp.sum((row < e).astype(jnp.int32))
            blks[8 * g + e] = jnp.minimum(first // 128, 2)

    def quarter(kt, group):
        rows = pl.ds(pl.multiple_of(256 * kt, 256), 256)

        def pairs(m, _):
            lefts, blocks = [], []
            for u in range(4):
                n = 4 * m + u
                e = n - 8 * group
                blk = blks[n]
                parts = []
                for b in range(2):
                    keep = id_all[group, blk + b] == e
                    parts.append(jnp.where(keep, x_all[group][blk + b, rows, :].astype(F32), 0.0).astype(BF16))
                lefts.append(jnp.concatenate(parts, axis=1))
                blocks.append(blk)
            for it in range(4):
                cols = pl.ds(256 * it, 256)
                total = sq[kt, :, cols]
                for u in range(4):
                    right = jnp.concatenate([y_all[group][blocks[u], :, cols], y_all[group][blocks[u] + 1, :, cols]], axis=0)
                    value = jnp.dot(lefts[u], right, preferred_element_type=F32).astype(BF16)
                    rot[4 * m + u, rows, cols] = value
                    wide = value.astype(F32)
                    total = total + wide * wide
                sq[kt, :, cols] = total
            return 0

        lax.fori_loop(2 * group, 2 * group + 2, pairs, 0)

    def sq_copy(kt):
        return remote(sq.at[kt], sq_got.at[kt], (sq_s, sq_r), kt, sibling)

    def add_up(kt):
        sq_copy(kt).wait()

        def chunk(i, _):
            part = pl.ds(pl.multiple_of(32 * i, 32), 32)
            sq[kt, part, :] = (sq[kt, part, :] + sq_got[kt, part, :]) * (1.0 / 32.0)
            return 0

        lax.fori_loop(0, 8, chunk, 0)
        c_stage[kt] = sq[kt, pl.ds(pl.multiple_of(128 * c, 128), 128), :].astype(BF16)

    def norms(g, total):
        wide_ids = [jnp.broadcast_to(id_all[g, b].astype(F32), (128, 128)) for b in range(4)]
        tall_ids = [wide.T for wide in wide_ids]
        for a in range(4):
            for b in range(4):
                part = pl.ds(128 * b, 128)
                if abs(a - b) > 1:
                    gram[0, pl.ds(128 * a, 128), part] = jnp.zeros((128, 128), BF16)
                    gram[1, pl.ds(128 * a, 128), part] = jnp.zeros((128, 128), BF16)
                    continue
                value = lax.dot_general(
                    y_all[g][a], y_all[g][b], (((1,), (1,)), ((), ())), preferred_element_type=F32)
                value = jnp.where(tall_ids[a] == wide_ids[b], value, 0.0)
                high = value.astype(BF16)
                gram[0, pl.ds(128 * a, 128), part] = high
                gram[1, pl.ds(128 * a, 128), part] = (value - high.astype(F32)).astype(BF16)

        def chunk(i, total):
            rows = pl.ds(pl.multiple_of(256 * i, 256), 256)
            left = jnp.concatenate([x_all[g][b, rows, :] for b in range(4)], axis=1)
            value = jnp.dot(left, gram[0], preferred_element_type=F32)
            value += jnp.dot(left, gram[1], preferred_element_type=F32)
            value = value * left.astype(F32)
            for b in range(4):
                total = total + jnp.sum(value[:, 128 * b:128 * b + 128].reshape(32, 8, 128), axis=0)
            return total

        return lax.fori_loop(0, 4, chunk, total)

    def slab(xv, hv):
        return corr.at[2 * xv + hv, pl.ds(pl.multiple_of(128 * c, 128), 128), :]

    def out_copies(j):
        copies = []
        for hd in range(2):
            if hd or j:
                copies.append(pltpu.make_async_remote_copy(
                    src_ref=c_stage.at[xs[j]], dst_ref=slab(x, h), send_sem=o_s.at[4 * hd + j],
                    recv_sem=o_r.at[4 * hd + j], device_id=device((h, oh)[hd], c, y, xs[j], z),
                    device_id_type=MESH))
        return copies

    own_out = pltpu.make_async_copy(c_stage.at[x], slab(x, h), loc.at[3])
    def at_y(v):
        return device(v // 2, c, lax.rem(v, 2), x, z)

    def over_x(d):
        return device(h, c, y, xs[d], z)

    def over_y(d):
        return at_y(ys[d])

    def over_z(d):
        return device(h, c, y, x, zs[d])

    def over_cores(d):
        return sibling

    class Spread:
        def __init__(self, value, axes, buf, got_buf, sems):
            self.value, self.axes, self.buf, self.got, self.sems, self.n = value, list(axes), buf, got_buf, sems, 0

        def start(self):
            n, (where, count) = self.n, self.axes[self.n]
            self.buf[n] = self.value
            self.copies = [
                go(remote(self.buf.at[n], self.got.at[n, d], self.sems, 3 * n + d, where(d + 1)))
                for d in range(count)]

        def wait(self):
            self.value = self.buf[self.n]
            for d, copy in enumerate(self.copies):
                copy.wait_recv()
                self.value = self.value + self.got[self.n, d]
            self.n += 1

    for copy in got[0]:
        copy.wait_recv()
    total = norms(0, jnp.zeros((8, 128), F32))
    for j in range(4):
        quarter(xs[j], 0)
    for copy in got[1]:
        copy.wait_recv()
    total = norms(1, total)
    whole = Spread(total, ((over_cores, 1), (over_x, 3), (over_y, 3), (over_z, 3)), red, red_got, (t_s, t_r))
    for j in range(4):
        whole.start()
        quarter(xs[j], 1)
        sq_copy(xs[j]).start()
        whole.wait()
        if j:
            add_up(xs[j - 1])
            for copy in out_copies(j - 1):
                copy.start()
            if j == 1:
                own_out.start()
    add_up(xs[3])
    for copy in out_copies(3):
        copy.start()
    damping = 0.5 * (jnp.sum(whole.value) * (1.0 / 32.0) / (float(D_IN) * float(D_OUT)))

    def second(kt):
        rows = pl.ds(pl.multiple_of(256 * kt, 256), 256)

        def invert(i, _):
            part = pl.ds(pl.multiple_of(32 * i, 32), 32)
            sq[kt, part, :] = 1.0 / (sq[kt, part, :] + damping)
            return 0

        lax.fori_loop(0, 8, invert, 0)

        def pairs(m, _):
            query_in = x_all[1][4, rows, :].astype(F32)
            sums = [None] * 4
            for it in range(4):
                cols = pl.ds(256 * it, 256)
                factor = sq[kt, :, cols]
                query_out = y_all[1][4, :, cols]
                for u in range(4):
                    cond = (rot[4 * m + u, rows, cols].astype(F32) * factor).astype(BF16)
                    part = lax.dot_general(
                        cond, query_out, (((1,), (1,)), ((), ())), preferred_element_type=F32)
                    sums[u] = part if it == 0 else sums[u] + part
            for u in range(4):
                acc[pl.ds(4 * m + u, 1), :] += jnp.sum(sums[u] * query_in, axis=0, keepdims=True)
            return 0

        lax.fori_loop(0, EX // 2, pairs, 0)

    def hand_on(xv, hv):
        return remote(slab(xv, hv), slab(xv, hv), (f_s, f_r), 2 * xv + hv, sibling)

    for j in range(4):
        second(xs[j])
        for copy in out_copies(j):
            copy.wait()
        if j == 0:
            own_out.wait()
        for hv in (h, oh):
            hand_on(xb[j], hv).start()
    result = Spread(acc[...], ((over_z, 3), (over_x, 3), (over_y, 3)), red2, red2_got, (p_s, p_r))
    for _ in range(3):
        result.start()
        result.wait()
    scores[...] = result.value
    for j in range(4):
        for hv in (h, oh):
            hand_on(xb[j], hv).wait()
    for copy in started:
        copy.wait_send()


def score(x_mine, y_mine, ids):
    dma = pltpu.SemaphoreType.DMA
    vmem = pl.BlockSpec(memory_space=pltpu.VMEM)
    return pl.pallas_call(
        score_kernel,
        out_shape=(jax.ShapeDtypeStruct((8, 256, 1024), BF16), jax.ShapeDtypeStruct((2 * EX, 128), F32)),
        in_specs=[vmem] * 3,
        out_specs=(pl.BlockSpec(memory_space=pltpu.VMEM), vmem),
        scratch_shapes=[
            (pltpu.VMEM((4, 1024, 128), BF16), pltpu.VMEM((5, 1024, 128), BF16)),
            (pltpu.VMEM((4, 128, 1024), BF16), pltpu.VMEM((5, 128, 1024), BF16)),
            pltpu.VMEM((2, 4, 1, 128), jnp.int32),
            pltpu.VMEM((2 * EX, 1024, 1024), BF16),
            pltpu.VMEM((4, 256, 1024), F32),
            pltpu.VMEM((4, 256, 1024), F32),
            pltpu.VMEM((4, 128, 1024), BF16),
            pltpu.VMEM((2 * EX, 128), F32),
            pltpu.VMEM((2, 512, 512), BF16),
            pltpu.VMEM((4, 8, 128), F32),
            pltpu.VMEM((4, 3, 8, 128), F32),
            pltpu.VMEM((3, 2 * EX, 128), F32),
            pltpu.VMEM((3, 3, 2 * EX, 128), F32),
            pltpu.SMEM((2 * EX,), jnp.int32),
            dma((6,)),
            dma((16,)), dma((16,)),
            dma((16,)), dma((16,)),
            dma((1,)), dma((1,)),
            dma((4,)), dma((4,)),
            dma((12,)), dma((12,)),
            dma((8,)), dma((8,)),
            dma((8,)), dma((8,)),
            dma((9,)), dma((9,)),
        ],
        compiler_params=pltpu.CompilerParams(
            collective_id=2, has_side_effects=True, vmem_limit_bytes=60 * 2**20),
        cost_estimate=pl.CostEstimate(flops=2 * 10**10, bytes_accessed=10**7, transcendentals=0),
        name="score",
    )(x_mine, y_mine, ids)


def widen_kernel(corr, out, stage, sems):
    def copy(n):
        yv, xv = n // 4, n % 4
        return pltpu.make_async_copy(stage.at[n % 4], out.at[:, pl.ds(1024 * (4 * yv + xv), 1024)], sems.at[n % 4])

    for n in range(8):
        yv, xv = n // 4, n % 4
        if n >= 4:
            copy(n - 4).wait()
        for zv in range(4):
            for hv in range(2):
                stage[n % 4, :, pl.ds(128 * (2 * zv + hv), 128)] = corr[
                    2 * xv + hv, :, pl.ds(128 * (2 * zv + yv), 128)].astype(F32)
        copy(n).start()
    for n in range(4, 8):
        copy(n).wait()


def widen(corr):
    return pl.pallas_call(
        widen_kernel,
        out_shape=jax.ShapeDtypeStruct((256, D_OUT), F32),
        in_specs=[pl.BlockSpec(memory_space=pltpu.VMEM)],
        out_specs=pl.BlockSpec(memory_space=pl.ANY),
        scratch_shapes=[pltpu.VMEM((4, 256, 1024), F32), pltpu.SemaphoreType.DMA((4,))],
        compiler_params=pltpu.CompilerParams(vmem_limit_bytes=60 * 2**20),
        name="widen",
    )(corr)


def per_device(activations, out_grads, query_acts, query_grads, eig_in, eig_out, example_ids):
    x_mine, y_mine = rotate(activations, out_grads, query_acts, query_grads, eig_in, eig_out)
    corr, sums = score(x_mine, y_mine, example_ids.reshape(4, 1, 128))
    h = lax.axis_index("dp") // 2
    mine = lax.dynamic_slice_in_dim(sums, EX * h, EX, 0)
    norm_factor = 1.0 / jnp.sqrt(jnp.float32(D_IN) * jnp.float32(D_OUT))
    scores = jnp.sum(mine.reshape(EX, NQ, QTOK), axis=2).T * norm_factor
    return widen(corr), scores


def solution(mesh):
    return jax.shard_map(
        per_device,
        mesh=mesh,
        in_specs=(
            P("dp", "fsdp"),
            P("dp", "fsdp"),
            P(None, "fsdp"),
            P(None, "fsdp"),
            P("fsdp", None),
            P("fsdp", None),
            P("dp", None),
        ),
        out_specs=(P("fsdp", None), P(None, "dp")),
        check_vma=False,
    )
```

time: 213 us -> 189 us (0.89)
  Pallas kernels: 211 us -> 186 us
    pallas_call x1, Pallas kernels: 102 us -> 85.9 us  [rotate(): pl.pallas_call(rotate_kernel, out_shape=(jax.ShapeDtypeStruct((9, 128, 12...]
    pallas_call x1, Pallas kernels: 102 us -> 94.6 us  [score(): pl.pallas_call(score_kernel, out_shape=(jax.ShapeDtypeStruct((8, 256, 102...]
where the time goes in v3:
time: 189 us; the launch traced here: 188 us
  Pallas kernels  186 us (98%)
    pallas_call x1, Pallas kernels, score(): pl.pallas_call(score_kernel, out_shape=(jax.ShapeDtypeStruct((8, 256, 102...  94.6 us
    pallas_call x1, Pallas kernels, rotate(): pl.pallas_call(rotate_kernel, out_shape=(jax.ShapeDtypeStruct((9, 128, 12...  85.9 us
    pallas_call x1, Pallas kernels, widen(): pl.pallas_call(widen_kernel, out_shape=jax.ShapeDtypeStruct((256, D_OUT),...  5.64 us

profile of v3, /device:TPU:0, one launch (start us, length us, event | category | flops | bytes accessed | tf_op | source)
XLA Modules:
  0.0 188.4 jit_solution(10158285663059740319)
XLA Ops:
  0.6 85.9 %rotate.1 = (bf16[9,128,128]{2,1,0:T(8,128)(2,1)}, bf16[9,128,128]{2,1,0:T(8,128)(2,1)}) custom-call(bf16[512,256]{1,0:T(8,128)(2,1)} %act.1, bf16[512,256]{1,0:T(8,128)(2,1)} %grd.1, bf16[128,256]{1,0:T(8,128)(2,1)} %qa.1, bf16[128,256]{1,0:T(8,128)(2,1)} %qg.1, bf16[256,8192]{1,0:T(8,128)(2,1)} %eig_in.1, bf16[256,8192]{1,0:T(8,128)(2,1)} %eig_out.1), custom_call_target="tpu_custom_call" | custom-call | flops 5000000000 | bytes 10000000 | tf_op jit(solution)/shard_map/rotate/pallas_call | solution.py:277
  86.5 94.6 %score.1 = (bf16[8,256,1024]{2,1,0:T(8,128)(2,1)}, f32[16,128]{1,0:T(8,128)}) custom-call(bf16[9,128,128]{2,1,0:T(8,128)(2,1)} %get-tuple-element.6.x_mine, bf16[9,128,128]{2,1,0:T(8,128)(2,1)} %get-tuple-element.7.y_mine, s32[4,1,128]{2,1,0:T(1,128)} %bitcast.5), custom_call_target="tpu_custom_call" | custom-call | flops 20000000000 | bytes 10000000 | tf_op jit(solution)/shard_map/score/pallas_call | solution.py:575
  181.1 0.7 constant_dynamic-slice_fusion
  181.8 0.1 copy.10
  182.0 0.7 copy.11
  182.6 5.6 %widen.1 = f32[256,8192]{1,0:T(8,128)} custom-call(bf16[8,256,1024]{2,1,0:T(8,128)(2,1)} %get-tuple-element.8.corr), custom_call_target="tpu_custom_call" | custom-call | tf_op jit(solution)/shard_map/widen/pallas_call | solution.py:631
  (2 shorter events, 0.0 us)

commit v4 on v3

--- a/solution.py
+++ b/solution.py
@@ -318,7 +318,7 @@
     greet(
         [sibling, device(h, c, oy, x, z), device(oh, c, oy, x, z)]
         + [device(h, c, y, xs[d], z) for d in (1, 2, 3)]
-        + [device(oh, c, y, xs[d], z) for d in (0, 1, 2, 3)]
+        + [device(oh, c, y, x, z)]
         + [device(h, c, y, x, zs[d]) for d in (1, 2, 3)]
     )
     started = []
@@ -449,15 +449,12 @@
     def slab(xv, hv):
         return corr.at[2 * xv + hv, pl.ds(pl.multiple_of(128 * c, 128), 128), :]
 
-    def out_copies(j):
-        copies = []
-        for hd in range(2):
-            if hd or j:
-                copies.append(pltpu.make_async_remote_copy(
-                    src_ref=c_stage.at[xs[j]], dst_ref=slab(x, h), send_sem=o_s.at[4 * hd + j],
-                    recv_sem=o_r.at[4 * hd + j], device_id=device((h, oh)[hd], c, y, xs[j], z),
-                    device_id_type=MESH))
-        return copies
+    def out_copy(j):
+        return remote(c_stage.at[xs[j]], slab(x, h), (o_s, o_r), j, device(h, c, y, xs[j], z))
+
+    def cross(j):
+        src = slab(xb[j], h) if j else c_stage.at[x]
+        return remote(src, slab(xb[j], h), (o_s, o_r), 4 + j, across_h)
 
     own_out = pltpu.make_async_copy(c_stage.at[x], slab(x, h), loc.at[3])
     def at_y(v):
@@ -509,13 +506,13 @@
         whole.wait()
         if j:
             add_up(xs[j - 1])
-            for copy in out_copies(j - 1):
-                copy.start()
             if j == 1:
+                cross(0).start()
                 own_out.start()
+            else:
+                out_copy(j - 1).start()
     add_up(xs[3])
-    for copy in out_copies(3):
-        copy.start()
+    out_copy(3).start()
     damping = 0.5 * (jnp.sum(whole.value) * (1.0 / 32.0) / (float(D_IN) * float(D_OUT)))
 
     def second(kt):
@@ -549,18 +546,37 @@
     def hand_on(xv, hv):
         return remote(slab(xv, hv), slab(xv, hv), (f_s, f_r), 2 * xv + hv, sibling)
 
-    for j in range(4):
-        second(xs[j])
-        for copy in out_copies(j):
-            copy.wait()
-        if j == 0:
+    def pass_on(j):
+        if j:
+            out_copy(j).wait()
+            cross(j).start()
+        else:
             own_out.wait()
-        for hv in (h, oh):
-            hand_on(xb[j], hv).start()
+        hand_on(xb[j], h).start()
+
+    def take(j):
+        cross(j).wait()
+        hand_on(xb[j], oh).start()
+
+    pass_on(1)
+    second(xs[0])
+    pass_on(2)
+    second(xs[1])
+    pass_on(3)
+    second(xs[2])
+    pass_on(0)
+    second(xs[3])
     result = Spread(acc[...], ((over_z, 3), (over_x, 3), (over_y, 3)), red2, red2_got, (p_s, p_r))
-    for _ in range(3):
-        result.start()
-        result.wait()
+    result.start()
+    take(0)
+    result.wait()
+    result.start()
+    take(1)
+    result.wait()
+    result.start()
+    take(2)
+    result.wait()
+    take(3)
     scores[...] = result.value
     for j in range(4):
         for hv in (h, oh):

time: 189 us -> 180 us (0.952)
  Pallas kernels: 186 us -> 176 us
    pallas_call x1, Pallas kernels: 94.6 us -> 84.8 us  [score(): pl.pallas_call(score_kernel, out_shape=(jax.ShapeDtypeStruct((8, 256, 102...]
where the time goes in v4:
time: 180 us; the launch traced here: 179 us
  Pallas kernels  176 us (98%)
    pallas_call x1, Pallas kernels, rotate(): pl.pallas_call(rotate_kernel, out_shape=(jax.ShapeDtypeStruct((9, 128, 12...  85.9 us
    pallas_call x1, Pallas kernels, score(): pl.pallas_call(score_kernel, out_shape=(jax.ShapeDtypeStruct((8, 256, 102...  84.8 us
    pallas_call x1, Pallas kernels, widen(): pl.pallas_call(widen_kernel, out_shape=jax.ShapeDtypeStruct((256, D_OUT),...  5.64 us

profile of v4, /device:TPU:0, one launch (start us, length us, event | category | flops | bytes accessed | tf_op | source)
XLA Modules:
  0.0 178.6 jit_solution(18279382290752950136)
XLA Ops:
  0.6 85.9 %rotate.1 = (bf16[9,128,128]{2,1,0:T(8,128)(2,1)}, bf16[9,128,128]{2,1,0:T(8,128)(2,1)}) custom-call(bf16[512,256]{1,0:T(8,128)(2,1)} %act.1, bf16[512,256]{1,0:T(8,128)(2,1)} %grd.1, bf16[128,256]{1,0:T(8,128)(2,1)} %qa.1, bf16[128,256]{1,0:T(8,128)(2,1)} %qg.1, bf16[256,8192]{1,0:T(8,128)(2,1)} %eig_in.1, bf16[256,8192]{1,0:T(8,128)(2,1)} %eig_out.1), custom_call_target="tpu_custom_call" | custom-call | flops 5000000000 | bytes 10000000 | tf_op jit(solution)/shard_map/rotate/pallas_call | solution.py:277
  86.5 84.8 %score.1 = (bf16[8,256,1024]{2,1,0:T(8,128)(2,1)}, f32[16,128]{1,0:T(8,128)}) custom-call(bf16[9,128,128]{2,1,0:T(8,128)(2,1)} %get-tuple-element.6.x_mine, bf16[9,128,128]{2,1,0:T(8,128)(2,1)} %get-tuple-element.7.y_mine, s32[4,1,128]{2,1,0:T(1,128)} %bitcast.5), custom_call_target="tpu_custom_call" | custom-call | flops 20000000000 | bytes 10000000 | tf_op jit(solution)/shard_map/score/pallas_call | solution.py:591
  171.3 0.7 constant_dynamic-slice_fusion
  172.0 0.1 copy.10
  172.2 0.7 copy.11
  172.8 5.6 %widen.1 = f32[256,8192]{1,0:T(8,128)} custom-call(bf16[8,256,1024]{2,1,0:T(8,128)(2,1)} %get-tuple-element.8.corr), custom_call_target="tpu_custom_call" | custom-call | tf_op jit(solution)/shard_map/widen/pallas_call | solution.py:647
  (2 shorter events, 0.0 us)

commit v5 on v4

--- a/solution.py
+++ b/solution.py
@@ -625,44 +625,58 @@
     )(x_mine, y_mine, ids)
 
 
-def widen_kernel(corr, out, stage, sems):
+def widen_kernel(corr, sums, out, scores, got, stage, got_sems, sems):
+    def fetch(xv):
+        return pltpu.make_async_copy(corr.at[pl.ds(2 * xv, 2)], got.at[pl.ds(2 * xv, 2)], got_sems.at[xv])
+
     def copy(n):
-        yv, xv = n // 4, n % 4
+        xv, yv = n // 2, n % 2
         return pltpu.make_async_copy(stage.at[n % 4], out.at[:, pl.ds(1024 * (4 * yv + xv), 1024)], sems.at[n % 4])
 
+    for xv in range(4):
+        fetch(xv).start()
     for n in range(8):
-        yv, xv = n // 4, n % 4
+        xv, yv = n // 2, n % 2
+        if yv == 0:
+            fetch(xv).wait()
         if n >= 4:
             copy(n - 4).wait()
         for zv in range(4):
             for hv in range(2):
-                stage[n % 4, :, pl.ds(128 * (2 * zv + hv), 128)] = corr[
+                stage[n % 4, :, pl.ds(128 * (2 * zv + hv), 128)] = got[
                     2 * xv + hv, :, pl.ds(128 * (2 * zv + yv), 128)].astype(F32)
         copy(n).start()
+    h = lax.axis_index("dp") // 2
+    token = lax.broadcasted_iota(jnp.int32, (NQ * QTOK, NQ), 0)
+    query = lax.broadcasted_iota(jnp.int32, (NQ * QTOK, NQ), 1)
+    member = (token // QTOK == query).astype(F32)
+    scores[...] = jnp.dot(
+        sums[pl.ds(pl.multiple_of(EX * h, EX), EX), :], member,
+        preferred_element_type=F32, precision=lax.Precision.HIGHEST) * (float(D_IN) * float(D_OUT)) ** -0.5
     for n in range(4, 8):
         copy(n).wait()
 
 
-def widen(corr):
+def widen(corr, sums):
     return pl.pallas_call(
         widen_kernel,
-        out_shape=jax.ShapeDtypeStruct((256, D_OUT), F32),
-        in_specs=[pl.BlockSpec(memory_space=pltpu.VMEM)],
-        out_specs=pl.BlockSpec(memory_space=pl.ANY),
-        scratch_shapes=[pltpu.VMEM((4, 256, 1024), F32), pltpu.SemaphoreType.DMA((4,))],
+        out_shape=(jax.ShapeDtypeStruct((256, D_OUT), F32), jax.ShapeDtypeStruct((EX, NQ), F32)),
+        in_specs=[pl.BlockSpec(memory_space=pl.ANY), pl.BlockSpec(memory_space=pltpu.VMEM)],
+        out_specs=(pl.BlockSpec(memory_space=pl.ANY), pl.BlockSpec(memory_space=pltpu.VMEM)),
+        scratch_shapes=[
+            pltpu.VMEM((8, 256, 1024), BF16), pltpu.VMEM((4, 256, 1024), F32),
+            pltpu.SemaphoreType.DMA((4,)), pltpu.SemaphoreType.DMA((4,)),
+        ],
         compiler_params=pltpu.CompilerParams(vmem_limit_bytes=60 * 2**20),
         name="widen",
-    )(corr)
+    )(corr, sums)
 
 
 def per_device(activations, out_grads, query_acts, query_grads, eig_in, eig_out, example_ids):
     x_mine, y_mine = rotate(activations, out_grads, query_acts, query_grads, eig_in, eig_out)
     corr, sums = score(x_mine, y_mine, example_ids.reshape(4, 1, 128))
-    h = lax.axis_index("dp") // 2
-    mine = lax.dynamic_slice_in_dim(sums, EX * h, EX, 0)
-    norm_factor = 1.0 / jnp.sqrt(jnp.float32(D_IN) * jnp.float32(D_OUT))
-    scores = jnp.sum(mine.reshape(EX, NQ, QTOK), axis=2).T * norm_factor
-    return widen(corr), scores
+    corrections, scores = widen(corr, sums)
+    return corrections, scores.T
 
 
 def solution(mesh):

time: 180 us -> 179 us (level)
  no operation moved by 1% of the time
where the time goes in v5:
time: 179 us; the launch traced here: 177 us
  Pallas kernels  177 us (99%)
    pallas_call x1, Pallas kernels, rotate(): pl.pallas_call(rotate_kernel, out_shape=(jax.ShapeDtypeStruct((9, 128, 12...  85.9 us
    pallas_call x1, Pallas kernels, score(): pl.pallas_call(score_kernel, out_shape=(jax.ShapeDtypeStruct((8, 256, 102...  84.8 us
    pallas_call x1, Pallas kernels, widen(): pl.pallas_call(widen_kernel, out_shape=(jax.ShapeDtypeStruct((256, D_OUT)...  5.99 us

profile of v5, /device:TPU:0, one launch (start us, length us, event | category | flops | bytes accessed | tf_op | source)
XLA Modules:
  0.0 177.5 jit_solution(9476843321881813550)
XLA Ops:
  0.6 85.9 %rotate.1 = (bf16[9,128,128]{2,1,0:T(8,128)(2,1)}, bf16[9,128,128]{2,1,0:T(8,128)(2,1)}) custom-call(bf16[512,256]{1,0:T(8,128)(2,1)} %act.1, bf16[512,256]{1,0:T(8,128)(2,1)} %grd.1, bf16[128,256]{1,0:T(8,128)(2,1)} %qa.1, bf16[128,256]{1,0:T(8,128)(2,1)} %qg.1, bf16[256,8192]{1,0:T(8,128)(2,1)} %eig_in.1, bf16[256,8192]{1,0:T(8,128)(2,1)} %eig_out.1), custom_call_target="tpu_custom_call" | custom-call | flops 5000000000 | bytes 10000000 | tf_op jit(solution)/shard_map/rotate/pallas_call | solution.py:277
  86.5 84.8 %score.1 = (bf16[8,256,1024]{2,1,0:T(8,128)(2,1)}, f32[16,128]{1,0:T(8,128)}) custom-call(bf16[9,128,128]{2,1,0:T(8,128)(2,1)} %get-tuple-element.8.x_mine, bf16[9,128,128]{2,1,0:T(8,128)(2,1)} %get-tuple-element.9.y_mine, s32[4,1,128]{2,1,0:T(1,128)} %bitcast.3), custom_call_target="tpu_custom_call" | custom-call | flops 20000000000 | bytes 10000000 | tf_op jit(solution)/shard_map/score/pallas_call | solution.py:591
  171.3 6.0 %widen.1 = (f32[256,8192]{1,0:T(8,128)}, f32[8,32]{1,0:T(8,128)}) custom-call(bf16[8,256,1024]{2,1,0:T(8,128)(2,1)} %get-tuple-element.10.corr, f32[16,128]{1,0:T(8,128)} %get-tuple-element.11.sums), custom_call_target="tpu_custom_call" | custom-call | tf_op jit(solution)/shard_map/widen/pallas_call | solution.py:661
